TPU v7x, 512 devices: a whole 4x8x8 slice. The times are simulated.
512 devices in a mesh: gx: 16 (over z, core), gy: 8 (over y), gz: 4 (over x).
Axes of the slice: x: 4, y: 8, z: 8, core: 2. Of those that a mesh axis runs over, the one named last changes fastest.
Arguments:
- source: float32 [32, 128, 1024], P('gz', 'gx', 'gy'), may hold values from -24 to 24
- decay_rate: float32 [32, 128, 1024], P('gz', 'gx', 'gy'), may hold values from 0.005 to 1
- dispersion: float32 [3, 32, 128, 1024], P(None, 'gz', 'gx', 'gy'), may hold values from 0.1 to 2
- velocity: float32 [3, 32, 128, 1024], P(None, 'gz', 'gx', 'gy'), may hold values from 0.1 to 2
- upwind: int32 [3, 32, 128, 1024], P(None, 'gz', 'gx', 'gy'), may hold values 0 or 1
Outputs:
- adjoint: float32 [32, 128, 1024], P('gz', 'gx', 'gy')
All inputs are finite; a program needn't handle non-finite values. No bound on the sum of `upwind` on one device may be relied on, other than what follows from the above.
Results may differ from a plain program's by a relative error of at most 0.0008.
Values sent between devices are 32-bit elements; how exact they have to be, the bound alone decides.
A program may use at most 128 MiB of HBM per device.

v0:
```python
import jax
import jax.numpy as jnp
from jax import lax
from jax.sharding import PartitionSpec as P

LEVELS = 3
SWEEPS = 2
COARSE_SWEEPS = 8


relax_weight = 0.7


def padded_2(block, sides, width):
    for axis, dim in sides:
        count = lax.axis_size(axis)
        forward = [(i, i + 1) for i in range(count - 1)]
        backward = [(target, source) for source, target in forward]
        low = lax.ppermute(
            lax.slice_in_dim(block, block.shape[dim] - width, None, axis=dim), axis, forward
        )
        high = lax.ppermute(lax.slice_in_dim(block, 0, width, axis=dim), axis, backward)
        block = jnp.concatenate([low, block, high], axis=dim)
    return block


def restrict_sum(values):
    dims = values.shape
    blocks = values.reshape(dims[0] // 2, 2, dims[1] // 2, 2, dims[2] // 2, 2)
    return blocks.sum(axis=(1, 3, 5))


def coarse_faces(values, direction, pick):
    dims = values.shape
    blocks = values.reshape(dims[0] // 2, 2, dims[1] // 2, 2, dims[2] // 2, 2)
    chosen = lax.slice_in_dim(blocks, pick, pick + 1, axis=2 * direction + 1)
    return chosen.sum(axis=(1, 3, 5))


def prolong_copy(coarse):
    dims = coarse.shape
    wide = jnp.broadcast_to(coarse[:, None, :, None, :, None], (dims[0], 2, dims[1], 2, dims[2], 2))
    return wide.reshape(2 * dims[0], 2 * dims[1], 2 * dims[2])


def apply_operator(values, padded, rates, upper_terms, lower_terms):
    nexts = (padded[2:, 1:-1, 1:-1], padded[1:-1, 2:, 1:-1], padded[1:-1, 1:-1, 2:])
    prevs = (padded[:-2, 1:-1, 1:-1], padded[1:-1, :-2, 1:-1], padded[1:-1, 1:-1, :-2])
    result = rates * values
    for direction in range(3):
        result = (
            result
            + upper_terms[direction] * (values - nexts[direction])
            + lower_terms[direction] * (values - prevs[direction])
        )
    return result


def diagonal_of(rates, upper_terms, lower_terms):
    total = rates
    for direction in range(3):
        total = total + upper_terms[direction] + lower_terms[direction]
    return total


def face_pair(k_ext, v_ext, f_ext, direction, positions, total):
    length = k_ext.shape[direction] - 2

    def part(array, begin):
        return lax.slice_in_dim(array, begin, begin + length, axis=direction)

    k_prev, k_here, k_next = (part(k_ext, 0), part(k_ext, 1), part(k_ext, 2))
    v_prev, v_here, v_next = (part(v_ext, 0), part(v_ext, 1), part(v_ext, 2))
    f_prev, f_here = (part(f_ext, 0), part(f_ext, 1))
    upper = jnp.where(
        positions == total - 1, 0.0, 0.5 * (k_here + k_next) + f_here * (0.5 * (v_here + v_next))
    )
    lower = jnp.where(
        positions == 0, 0.0, 0.5 * (k_prev + k_here) + (1.0 - f_prev) * (0.5 * (v_prev + v_here))
    )
    return (upper, lower)


def build_levels(rates, uppers, lowers):
    levels = []
    for depth in range(LEVELS + 1):
        levels.append((rates, uppers, lowers, diagonal_of(rates, uppers, lowers)))
        if depth < LEVELS:
            rates = restrict_sum(rates)
            uppers = [coarse_faces(uppers[direction], direction, 1) for direction in range(3)]
            lowers = [coarse_faces(lowers[direction], direction, 0) for direction in range(3)]
    return levels


def sweeps(rhs, level, start, steps_count, neighbours):
    rates, upper_terms, lower_terms, diagonal = level
    current = start
    for step in range(steps_count):
        if current is None:
            current = relax_weight * rhs / diagonal
        else:
            image = apply_operator(current, neighbours(current), rates, upper_terms, lower_terms)
            current = current + relax_weight * (rhs - image) / diagonal
    return current


def cycle(rhs, levels, depth, neighbours, coarsest):
    if depth == len(levels) - 1:
        return coarsest(rhs)
    level = levels[depth]
    current = sweeps(rhs, level, None, SWEEPS, neighbours)
    residual = rhs - apply_operator(current, neighbours(current), level[0], level[1], level[2])
    correction = cycle(restrict_sum(residual), levels, depth + 1, neighbours, coarsest)
    current = current + prolong_copy(correction)
    return sweeps(rhs, level, current, SWEEPS, neighbours)


def fine_rim(values):
    return padded_2(values, (("gx", 1), ("gy", 2), ("gz", 0)), 1)


def on_device(source, decay_rate, dispersion, velocity, upwind):
    flags = upwind.astype(jnp.float32)
    places = (lax.axis_index("gz"), lax.axis_index("gx"), lax.axis_index("gy"))
    counts = (lax.axis_size("gz"), lax.axis_size("gx"), lax.axis_size("gy"))
    stacked = jnp.concatenate([dispersion, velocity, flags], axis=0)
    grown = padded_2(stacked, (("gx", 2), ("gy", 3), ("gz", 1)), 1)
    triples = []
    for direction in range(3):
        inner = [slice(1, -1), slice(1, -1), slice(1, -1)]
        inner[direction] = slice(None)
        view = grown[(slice(None),) + tuple(inner)]
        triples.append((view[direction], view[3 + direction], view[6 + direction]))
    uppers, lowers = ([], [])
    for direction in range(3):
        length = source.shape[direction]
        positions = (
            lax.broadcasted_iota(jnp.int32, source.shape, direction) + places[direction] * length
        )
        trio = triples[direction]
        upper, lower = face_pair(
            trio[0], trio[1], trio[2], direction, positions, length * counts[direction]
        )
        uppers.append(upper)
        lowers.append(lower)
    levels = build_levels(decay_rate, uppers, lowers)
    last = levels[LEVELS]

    def coarse_rim(values):
        return padded_2(values, (("gx", 1), ("gy", 2), ("gz", 0)), 1)

    def coarsest(rhs):
        return sweeps(rhs, last, None, COARSE_SWEEPS, coarse_rim)

    return cycle(source, levels, 0, fine_rim, coarsest)


def solution(mesh):
    in_specs = (
        P("gz", "gx", "gy"),
        P("gz", "gx", "gy"),
        P(None, "gz", "gx", "gy"),
        P(None, "gz", "gx", "gy"),
        P(None, "gz", "gx", "gy"),
    )
    out_specs = P("gz", "gx", "gy")
    return jax.shard_map(
        on_device, mesh=mesh, in_specs=in_specs, out_specs=out_specs, check_vma=False
    )
```

profile of v0, /device:TPU:1, one launch (start us, length us, event | category | flops | bytes accessed | tf_op | source)
XLA Modules:
  0.0 528.0 jit_solution(13632067920654938318)
XLA Ops:
  2.0 5.4 %collective-permute-start = (f32[9,8,1,128]{3,2,1,0:T(1,128)S(1)}, f32[9,8,1,128]{3,2,1,0:T(1,128)S(1)}, u32[]{:S(2)}, u32[]{:S(2)}) collective-permute-start(f32[9,8,1,128]{3,2,1,0:T(1,128)S(1)} %get-tuple-element.25), channel_id=1, source_target_pairs={{0,32},{32,64},{64,96},{96,128},{128,160},{160,192},{192,224},{224... | collective-permute-start | bytes 110600 | tf_op jit(solution)/shard_map/ppermute | solution.py:19
  7.4 4.7 collective-permute-start.1
  21.1 3.2 collective-permute-done.3
  26.4 4.0 collective-permute-start.5
  34.7 4.6 collective-permute-start.6
  41.4 3.4 add.723
  44.8 3.4 add.725
  53.4 3.4 reshape.264
  61.2 3.2 collective-permute-start.8
  66.2 4.2 collective-permute-done.9
  71.8 4.7 collective-permute-start.11
  77.6 6.1 %collective-permute-start.12 = (f32[8,1,128]{2,1,0:T(1,128)S(1)}, f32[8,1,128]{2,1,0:T(1,128)S(1)}, u32[]{:S(2)}, u32[]{:S(2)}) collective-permute-start(f32[8,1,128]{2,1,0:T(1,128)S(1)} %get-tuple-element.55), channel_id=1, source_target_pairs={{0,32},{32,64},{64,96},{96,128},{128,160},{160,192},{192,224},{224... | collective-permute-start | bytes 12296 | tf_op jit(solution)/shard_map/ppermute | solution.py:19
  88.8 4.4 collective-permute-start.14
  94.9 3.3 collective-permute-done.15
  99.6 4.8 collective-permute-start.17
  107.5 4.2 collective-permute-start.18
  116.8 3.4 collective-permute-start.20
  121.5 3.2 collective-permute-done.21
  126.1 4.7 collective-permute-start.23
  131.6 5.2 collective-permute-start.24
  146.1 3.2 collective-permute-done.27
  150.7 4.5 collective-permute-start.29
  156.5 6.6 %collective-permute-start.30 = (f32[2,1,32]{2,1,0:T(1,128)S(1)}, f32[2,1,32]{2,1,0:T(1,128)S(1)}, u32[]{:S(2)}, u32[]{:S(2)}) collective-permute-start(f32[2,1,32]{2,1,0:T(1,128)S(1)} %get-tuple-element.111), channel_id=1, source_target_pairs={{0,32},{32,64},{64,96},{96,128},{128,160},{160,192},{192,224},{224... | collective-permute-start | bytes 776 | tf_op jit(solution)/shard_map/ppermute | solution.py:19
  172.2 3.0 collective-permute-done.33
  176.6 4.5 collective-permute-start.35
  182.0 5.5 %collective-permute-start.36 = (f32[2,1,32]{2,1,0:T(1,128)S(1)}, f32[2,1,32]{2,1,0:T(1,128)S(1)}, u32[]{:S(2)}, u32[]{:S(2)}) collective-permute-start(f32[2,1,32]{2,1,0:T(1,128)S(1)} %get-tuple-element.109), channel_id=1, source_target_pairs={{0,32},{32,64},{64,96},{96,128},{128,160},{160,192},{192,224},{224... | collective-permute-start | bytes 776 | tf_op jit(solution)/shard_map/ppermute | solution.py:19
  196.6 3.0 collective-permute-done.39
  201.0 4.5 collective-permute-start.41
  206.6 5.4 %collective-permute-start.42 = (f32[1,1,16]{2,1,0:T(1,128)S(1)}, f32[1,1,16]{2,1,0:T(1,128)S(1)}, u32[]{:S(2)}, u32[]{:S(2)}) collective-permute-start(f32[1,1,16]{2,1,0:T(1,128)S(1)} %get-tuple-element.5), channel_id=1, source_target_pairs={{0,32},{32,64},{64,96},{96,128},{128,160},{160,192},{192,224},{224... | collective-permute-start | bytes 200 | tf_op jit(solution)/shard_map/ppermute | solution.py:19
  221.2 3.0 collective-permute-done.45
  225.6 4.5 collective-permute-start.47
  230.9 5.4 %collective-permute-start.48 = (f32[1,1,16]{2,1,0:T(1,128)S(1)}, f32[1,1,16]{2,1,0:T(1,128)S(1)}, u32[]{:S(2)}, u32[]{:S(2)}) collective-permute-start(f32[1,1,16]{2,1,0:T(1,128)S(1)} %divide_add_fusion.8), channel_id=1, source_target_pairs={{0,32},{32,64},{64,96},{96,128},{128,160},{160,192},{192,224},{224... | collective-permute-start | bytes 200 | tf_op jit(solution)/shard_map/ppermute | solution.py:19
  245.5 3.0 collective-permute-done.51
  249.8 4.5 collective-permute-start.53
  255.2 5.5 %collective-permute-start.54 = (f32[1,1,16]{2,1,0:T(1,128)S(1)}, f32[1,1,16]{2,1,0:T(1,128)S(1)}, u32[]{:S(2)}, u32[]{:S(2)}) collective-permute-start(f32[1,1,16]{2,1,0:T(1,128)S(1)} %divide_add_fusion.7), channel_id=1, source_target_pairs={{0,32},{32,64},{64,96},{96,128},{128,160},{160,192},{192,224},{224... | collective-permute-start | bytes 200 | tf_op jit(solution)/shard_map/ppermute | solution.py:19
  274.1 4.5 collective-permute-start.59
  279.5 5.5 %collective-permute-start.60 = (f32[1,1,16]{2,1,0:T(1,128)S(1)}, f32[1,1,16]{2,1,0:T(1,128)S(1)}, u32[]{:S(2)}, u32[]{:S(2)}) collective-permute-start(f32[1,1,16]{2,1,0:T(1,128)S(1)} %divide_add_fusion.6), channel_id=1, source_target_pairs={{0,32},{32,64},{64,96},{96,128},{128,160},{160,192},{192,224},{224... | collective-permute-start | bytes 200 | tf_op jit(solution)/shard_map/ppermute | solution.py:19
  294.0 3.0 collective-permute-done.63
  298.4 4.5 collective-permute-start.65
  303.8 5.5 %collective-permute-start.66 = (f32[1,1,16]{2,1,0:T(1,128)S(1)}, f32[1,1,16]{2,1,0:T(1,128)S(1)}, u32[]{:S(2)}, u32[]{:S(2)}) collective-permute-start(f32[1,1,16]{2,1,0:T(1,128)S(1)} %divide_add_fusion.5), channel_id=1, source_target_pairs={{0,32},{32,64},{64,96},{96,128},{128,160},{160,192},{192,224},{224... | collective-permute-start | bytes 200 | tf_op jit(solution)/shard_map/ppermute | solution.py:19
  318.3 3.0 collective-permute-done.69
  322.7 4.5 collective-permute-start.71
  328.1 5.5 %collective-permute-start.72 = (f32[1,1,16]{2,1,0:T(1,128)S(1)}, f32[1,1,16]{2,1,0:T(1,128)S(1)}, u32[]{:S(2)}, u32[]{:S(2)}) collective-permute-start(f32[1,1,16]{2,1,0:T(1,128)S(1)} %divide_add_fusion.4), channel_id=1, source_target_pairs={{0,32},{32,64},{64,96},{96,128},{128,160},{160,192},{192,224},{224... | collective-permute-start | bytes 200 | tf_op jit(solution)/shard_map/ppermute | solution.py:19
  347.0 4.5 collective-permute-start.77
  352.4 5.5 %collective-permute-start.78 = (f32[1,1,16]{2,1,0:T(1,128)S(1)}, f32[1,1,16]{2,1,0:T(1,128)S(1)}, u32[]{:S(2)}, u32[]{:S(2)}) collective-permute-start(f32[1,1,16]{2,1,0:T(1,128)S(1)} %divide_add_fusion.3), channel_id=1, source_target_pairs={{0,32},{32,64},{64,96},{96,128},{128,160},{160,192},{192,224},{224... | collective-permute-start | bytes 200 | tf_op jit(solution)/shard_map/ppermute | solution.py:19
  371.3 4.5 collective-permute-start.83
  376.9 5.5 %collective-permute-start.84 = (f32[2,1,32]{2,1,0:T(1,128)S(1)}, f32[2,1,32]{2,1,0:T(1,128)S(1)}, u32[]{:S(2)}, u32[]{:S(2)}) collective-permute-start(f32[2,1,32]{2,1,0:T(1,128)S(1)} %get-tuple-element.93), channel_id=1, source_target_pairs={{0,32},{32,64},{64,96},{96,128},{128,160},{160,192},{192,224},{224... | collective-permute-start | bytes 776 | tf_op jit(solution)/shard_map/ppermute | solution.py:19
  391.5 3.0 collective-permute-done.87
  395.9 4.5 collective-permute-start.89
  401.3 5.5 %collective-permute-start.90 = (f32[2,1,32]{2,1,0:T(1,128)S(1)}, f32[2,1,32]{2,1,0:T(1,128)S(1)}, u32[]{:S(2)}, u32[]{:S(2)}) collective-permute-start(f32[2,1,32]{2,1,0:T(1,128)S(1)} %get-tuple-element.91), channel_id=1, source_target_pairs={{0,32},{32,64},{64,96},{96,128},{128,160},{160,192},{192,224},{224... | collective-permute-start | bytes 776 | tf_op jit(solution)/shard_map/ppermute | solution.py:19
  415.9 3.0 collective-permute-done.93
  420.3 4.5 collective-permute-start.95
  425.9 5.5 %collective-permute-start.96 = (f32[4,1,64]{2,1,0:T(1,128)S(1)}, f32[4,1,64]{2,1,0:T(1,128)S(1)}, u32[]{:S(2)}, u32[]{:S(2)}) collective-permute-start(f32[4,1,64]{2,1,0:T(1,128)S(1)} %get-tuple-element.69), channel_id=1, source_target_pairs={{0,32},{32,64},{64,96},{96,128},{128,160},{160,192},{192,224},{224... | collective-permute-start | bytes 3080 | tf_op jit(solution)/shard_map/ppermute | solution.py:19
  440.6 3.2 collective-permute-done.99
  445.1 4.5 collective-permute-start.101
  450.5 5.5 %collective-permute-start.102 = (f32[4,1,64]{2,1,0:T(1,128)S(1)}, f32[4,1,64]{2,1,0:T(1,128)S(1)}, u32[]{:S(2)}, u32[]{:S(2)}) collective-permute-start(f32[4,1,64]{2,1,0:T(1,128)S(1)} %get-tuple-element.67), channel_id=1, source_target_pairs={{0,32},{32,64},{64,96},{96,128},{128,160},{160,192},{192,224},{224... | collective-permute-start | bytes 3080 | tf_op jit(solution)/shard_map/ppermute | solution.py:19
  465.2 3.2 collective-permute-done.105
  469.7 4.5 collective-permute-start.107
  476.7 5.5 %collective-permute-start.108 = (f32[8,1,128]{2,1,0:T(1,128)S(1)}, f32[8,1,128]{2,1,0:T(1,128)S(1)}, u32[]{:S(2)}, u32[]{:S(2)}) collective-permute-start(f32[8,1,128]{2,1,0:T(1,128)S(1)} %get-tuple-element.53), channel_id=1, source_target_pairs={{0,32},{32,64},{64,96},{96,128},{128,160},{160,192},{192,224},{224... | collective-permute-start | bytes 12296 | tf_op jit(solution)/shard_map/ppermute | solution.py:19
  491.3 3.7 collective-permute-done.111
  496.4 4.5 collective-permute-start.113
  502.0 5.4 %collective-permute-start.114 = (f32[8,1,128]{2,1,0:T(1,128)S(1)}, f32[8,1,128]{2,1,0:T(1,128)S(1)}, u32[]{:S(2)}, u32[]{:S(2)}) collective-permute-start(f32[8,1,128]{2,1,0:T(1,128)S(1)} %get-tuple-element.51), channel_id=1, source_target_pairs={{0,32},{32,64},{64,96},{96,128},{128,160},{160,192},{192,224},{224... | collective-permute-start | bytes 12296 | tf_op jit(solution)/shard_map/ppermute | solution.py:19
  516.6 3.7 collective-permute-done.117
  521.7 4.7 collective-permute-start.119
  (371 shorter events, 245.6 us)
Async XLA Ops:
  2.0 14.4 %collective-permute-start = (f32[9,8,1,128]{3,2,1,0:T(1,128)S(1)}, f32[9,8,1,128]{3,2,1,0:T(1,128)S(1)}, u32[]{:S(2)}, u32[]{:S(2)}) collective-permute-start(f32[9,8,1,128]{3,2,1,0:T(1,128)S(1)} %get-tuple-element.25), channel_id=1, source_target_pairs={{0,32},{32,64},{64,96},{96,128},{128,160},{160,192},{192,224},{224... | collective-permute-start | bytes 110600 | tf_op jit(solution)/shard_map/ppermute | solution.py:19
  7.4 9.1 %collective-permute-start.1 = (f32[9,8,1,128]{3,2,1,0:T(1,128)S(1)}, f32[9,8,1,128]{3,2,1,0:T(1,128)S(1)}, u32[]{:S(2)}, u32[]{:S(2)}) collective-permute-start(f32[9,8,1,128]{3,2,1,0:T(1,128)S(1)} %get-tuple-element.26), channel_id=1, source_target_pairs={{32,0},{64,32},{96,64},{128,96},{160,128},{192,160},{224,192},{256... | collective-permute-start | bytes 110600 | tf_op jit(solution)/shard_map/ppermute | solution.py:22
  25.1 6.9 %collective-permute-start.4 = (f32[9,1,10,130]{3,2,1,0:T(8,128)S(1)}, f32[9,1,10,130]{3,2,1,0:T(8,128)S(1)}, u32[]{:S(2)}, u32[]{:S(2)}) collective-permute-start(f32[9,1,10,130]{3,2,1,0:T(8,128)S(1)} %get-tuple-element.18), channel_id=1, source_target_pairs={{1,0},{2,1},{3,2},{5,4},{6,5},{7,6},{9,8},{10,9},{11,10},{13,12},{... | collective-permute-start | bytes 140408 | tf_op jit(solution)/shard_map/ppermute | solution.py:22
  26.4 6.5 %collective-permute-start.5 = (f32[9,1,10,130]{3,2,1,0:T(8,128)S(1)}, f32[9,1,10,130]{3,2,1,0:T(8,128)S(1)}, u32[]{:S(2)}, u32[]{:S(2)}) collective-permute-start(f32[9,1,10,130]{3,2,1,0:T(8,128)S(1)} %get-tuple-element.19), channel_id=1, source_target_pairs={{0,1},{1,2},{2,3},{4,5},{5,6},{6,7},{8,9},{9,10},{10,11},{12,13},{... | collective-permute-start | bytes 140408 | tf_op jit(solution)/shard_map/ppermute | solution.py:19
  34.7 26.4 %collective-permute-start.6 = (f32[8,1,128]{2,1,0:T(1,128)S(1)}, f32[8,1,128]{2,1,0:T(1,128)S(1)}, u32[]{:S(2)}, u32[]{:S(2)}) collective-permute-start(f32[8,1,128]{2,1,0:T(1,128)S(1)} %get-tuple-element.57), channel_id=1, source_target_pairs={{0,32},{32,64},{64,96},{96,128},{128,160},{160,192},{192,224},{224... | collective-permute-start | bytes 12296 | tf_op jit(solution)/shard_map/ppermute | solution.py:19
  39.2 21.8 %collective-permute-start.7 = (f32[8,1,128]{2,1,0:T(1,128)S(1)}, f32[8,1,128]{2,1,0:T(1,128)S(1)}, u32[]{:S(2)}, u32[]{:S(2)}) collective-permute-start(f32[8,1,128]{2,1,0:T(1,128)S(1)} %get-tuple-element.58), channel_id=1, source_target_pairs={{32,0},{64,32},{96,64},{128,96},{160,128},{192,160},{224,192},{256... | collective-permute-start | bytes 12296 | tf_op jit(solution)/shard_map/ppermute | solution.py:22
  64.4 6.0 %collective-permute-start.9 = (f32[8,10,1]{2,1,0:T(8,128)S(1)}, f32[8,10,1]{2,1,0:T(8,128)S(1)}, u32[]{:S(2)}, u32[]{:S(2)}) collective-permute-start(f32[8,10,1]{2,1,0:T(8,128)S(1)} %get-tuple-element.41), channel_id=1, source_target_pairs={{4,0},{8,4},{12,8},{16,12},{20,16},{24,20},{28,24},{5,1},{9,5},{13... | collective-permute-start | bytes 968 | tf_op jit(solution)/shard_map/ppermute | solution.py:22
  70.5 6.4 %collective-permute-start.10 = (f32[1,10,130]{2,1,0:T(8,128)S(1)}, f32[1,10,130]{2,1,0:T(8,128)S(1)}, u32[]{:S(2)}, u32[]{:S(2)}) collective-permute-start(f32[1,10,130]{2,1,0:T(8,128)S(1)} %get-tuple-element.33), channel_id=1, source_target_pairs={{1,0},{2,1},{3,2},{5,4},{6,5},{7,6},{9,8},{10,9},{11,10},{13,12},{... | collective-permute-start | bytes 15608 | tf_op jit(solution)/shard_map/ppermute | solution.py:22
  71.8 5.6 %collective-permute-start.11 = (f32[1,10,130]{2,1,0:T(8,128)S(1)}, f32[1,10,130]{2,1,0:T(8,128)S(1)}, u32[]{:S(2)}, u32[]{:S(2)}) collective-permute-start(f32[1,10,130]{2,1,0:T(8,128)S(1)} %get-tuple-element.34), channel_id=1, source_target_pairs={{0,1},{1,2},{2,3},{4,5},{5,6},{6,7},{8,9},{9,10},{10,11},{12,13},{... | collective-permute-start | bytes 15608 | tf_op jit(solution)/shard_map/ppermute | solution.py:19
  77.6 8.6 %collective-permute-start.12 = (f32[8,1,128]{2,1,0:T(1,128)S(1)}, f32[8,1,128]{2,1,0:T(1,128)S(1)}, u32[]{:S(2)}, u32[]{:S(2)}) collective-permute-start(f32[8,1,128]{2,1,0:T(1,128)S(1)} %get-tuple-element.55), channel_id=1, source_target_pairs={{0,32},{32,64},{64,96},{96,128},{128,160},{160,192},{192,224},{224... | collective-permute-start | bytes 12296 | tf_op jit(solution)/shard_map/ppermute | solution.py:19
  88.8 6.1 %collective-permute-start.14 = (f32[8,10,1]{2,1,0:T(8,128)S(1)}, f32[8,10,1]{2,1,0:T(8,128)S(1)}, u32[]{:S(2)}, u32[]{:S(2)}) collective-permute-start(f32[8,10,1]{2,1,0:T(8,128)S(1)} %get-tuple-element.40), channel_id=1, source_target_pairs={{0,4},{4,8},{8,12},{12,16},{16,20},{20,24},{24,28},{1,5},{5,9},{9,... | collective-permute-start | bytes 968 | tf_op jit(solution)/shard_map/ppermute | solution.py:19
  98.3 6.5 %collective-permute-start.16 = (f32[1,10,130]{2,1,0:T(8,128)S(1)}, f32[1,10,130]{2,1,0:T(8,128)S(1)}, u32[]{:S(2)}, u32[]{:S(2)}) collective-permute-start(f32[1,10,130]{2,1,0:T(8,128)S(1)} %get-tuple-element.31), channel_id=1, source_target_pairs={{1,0},{2,1},{3,2},{5,4},{6,5},{7,6},{9,8},{10,9},{11,10},{13,12},{... | collective-permute-start | bytes 15608 | tf_op jit(solution)/shard_map/ppermute | solution.py:22
  99.6 5.4 %collective-permute-start.17 = (f32[1,10,130]{2,1,0:T(8,128)S(1)}, f32[1,10,130]{2,1,0:T(8,128)S(1)}, u32[]{:S(2)}, u32[]{:S(2)}) collective-permute-start(f32[1,10,130]{2,1,0:T(8,128)S(1)} %get-tuple-element.32), channel_id=1, source_target_pairs={{0,1},{1,2},{2,3},{4,5},{5,6},{6,7},{8,9},{9,10},{10,11},{12,13},{... | collective-permute-start | bytes 15608 | tf_op jit(solution)/shard_map/ppermute | solution.py:19
  107.5 6.5 %collective-permute-start.18 = (f32[4,1,64]{2,1,0:T(1,128)S(1)}, f32[4,1,64]{2,1,0:T(1,128)S(1)}, u32[]{:S(2)}, u32[]{:S(2)}) collective-permute-start(f32[4,1,64]{2,1,0:T(1,128)S(1)} %get-tuple-element.73), channel_id=1, source_target_pairs={{0,32},{32,64},{64,96},{96,128},{128,160},{160,192},{192,224},{224... | collective-permute-start | bytes 3080 | tf_op jit(solution)/shard_map/ppermute | solution.py:19
  124.8 6.2 %collective-permute-start.22 = (f32[1,6,66]{2,1,0:T(8,128)S(1)}, f32[1,6,66]{2,1,0:T(8,128)S(1)}, u32[]{:S(2)}, u32[]{:S(2)}) collective-permute-start(f32[1,6,66]{2,1,0:T(8,128)S(1)} %get-tuple-element.49), channel_id=1, source_target_pairs={{1,0},{2,1},{3,2},{5,4},{6,5},{7,6},{9,8},{10,9},{11,10},{13,12},{... | collective-permute-start | bytes 4760 | tf_op jit(solution)/shard_map/ppermute | solution.py:22
  126.1 5.4 %collective-permute-start.23 = (f32[1,6,66]{2,1,0:T(8,128)S(1)}, f32[1,6,66]{2,1,0:T(8,128)S(1)}, u32[]{:S(2)}, u32[]{:S(2)}) collective-permute-start(f32[1,6,66]{2,1,0:T(8,128)S(1)} %get-tuple-element.50), channel_id=1, source_target_pairs={{0,1},{1,2},{2,3},{4,5},{5,6},{6,7},{8,9},{9,10},{10,11},{12,13},{... | collective-permute-start | bytes 4760 | tf_op jit(solution)/shard_map/ppermute | solution.py:19
  131.6 7.3 %collective-permute-start.24 = (f32[4,1,64]{2,1,0:T(1,128)S(1)}, f32[4,1,64]{2,1,0:T(1,128)S(1)}, u32[]{:S(2)}, u32[]{:S(2)}) collective-permute-start(f32[4,1,64]{2,1,0:T(1,128)S(1)} %get-tuple-element.71), channel_id=1, source_target_pairs={{0,32},{32,64},{64,96},{96,128},{128,160},{160,192},{192,224},{224... | collective-permute-start | bytes 3080 | tf_op jit(solution)/shard_map/ppermute | solution.py:19
  149.4 6.1 %collective-permute-start.28 = (f32[1,6,66]{2,1,0:T(8,128)S(1)}, f32[1,6,66]{2,1,0:T(8,128)S(1)}, u32[]{:S(2)}, u32[]{:S(2)}) collective-permute-start(f32[1,6,66]{2,1,0:T(8,128)S(1)} %get-tuple-element.47), channel_id=1, source_target_pairs={{1,0},{2,1},{3,2},{5,4},{6,5},{7,6},{9,8},{10,9},{11,10},{13,12},{... | collective-permute-start | bytes 4760 | tf_op jit(solution)/shard_map/ppermute | solution.py:22
  150.7 5.3 collective-permute-start.29
  156.5 8.7 %collective-permute-start.30 = (f32[2,1,32]{2,1,0:T(1,128)S(1)}, f32[2,1,32]{2,1,0:T(1,128)S(1)}, u32[]{:S(2)}, u32[]{:S(2)}) collective-permute-start(f32[2,1,32]{2,1,0:T(1,128)S(1)} %get-tuple-element.111), channel_id=1, source_target_pairs={{0,32},{32,64},{64,96},{96,128},{128,160},{160,192},{192,224},{224... | collective-permute-start | bytes 776 | tf_op jit(solution)/shard_map/ppermute | solution.py:19
  175.3 6.0 %collective-permute-start.34 = (f32[1,4,34]{2,1,0:T(4,128)S(1)}, f32[1,4,34]{2,1,0:T(4,128)S(1)}, u32[]{:S(2)}, u32[]{:S(2)}) collective-permute-start(f32[1,4,34]{2,1,0:T(4,128)S(1)} %get-tuple-element.87), channel_id=1, source_target_pairs={{1,0},{2,1},{3,2},{5,4},{6,5},{7,6},{9,8},{10,9},{11,10},{13,12},{... | collective-permute-start | bytes 1640 | tf_op jit(solution)/shard_map/ppermute | solution.py:22
  176.6 5.3 collective-permute-start.35
  182.0 7.6 %collective-permute-start.36 = (f32[2,1,32]{2,1,0:T(1,128)S(1)}, f32[2,1,32]{2,1,0:T(1,128)S(1)}, u32[]{:S(2)}, u32[]{:S(2)}) collective-permute-start(f32[2,1,32]{2,1,0:T(1,128)S(1)} %get-tuple-element.109), channel_id=1, source_target_pairs={{0,32},{32,64},{64,96},{96,128},{128,160},{160,192},{192,224},{224... | collective-permute-start | bytes 776 | tf_op jit(solution)/shard_map/ppermute | solution.py:19
  199.7 5.9 %collective-permute-start.40 = (f32[1,4,34]{2,1,0:T(4,128)S(1)}, f32[1,4,34]{2,1,0:T(4,128)S(1)}, u32[]{:S(2)}, u32[]{:S(2)}) collective-permute-start(f32[1,4,34]{2,1,0:T(4,128)S(1)} %get-tuple-element.83), channel_id=1, source_target_pairs={{1,0},{2,1},{3,2},{5,4},{6,5},{7,6},{9,8},{10,9},{11,10},{13,12},{... | collective-permute-start | bytes 1640 | tf_op jit(solution)/shard_map/ppermute | solution.py:22
  201.0 5.3 collective-permute-start.41
  206.6 7.4 %collective-permute-start.42 = (f32[1,1,16]{2,1,0:T(1,128)S(1)}, f32[1,1,16]{2,1,0:T(1,128)S(1)}, u32[]{:S(2)}, u32[]{:S(2)}) collective-permute-start(f32[1,1,16]{2,1,0:T(1,128)S(1)} %get-tuple-element.5), channel_id=1, source_target_pairs={{0,32},{32,64},{64,96},{96,128},{128,160},{160,192},{192,224},{224... | collective-permute-start | bytes 200 | tf_op jit(solution)/shard_map/ppermute | solution.py:19
  224.3 5.9 %collective-permute-start.46 = (f32[1,3,18]{2,1,0:T(4,128)S(1)}, f32[1,3,18]{2,1,0:T(4,128)S(1)}, u32[]{:S(2)}, u32[]{:S(2)}) collective-permute-start(f32[1,3,18]{2,1,0:T(4,128)S(1)} %pad_maximum_fusion.286), channel_id=1, source_target_pairs={{1,0},{2,1},{3,2},{5,4},{6,5},{7,6},{9,8},{10,9},{11,10},{13,12},{... | collective-permute-start | bytes 656 | tf_op jit(solution)/shard_map/ppermute | solution.py:22
  225.6 5.3 collective-permute-start.47
  230.9 7.4 %collective-permute-start.48 = (f32[1,1,16]{2,1,0:T(1,128)S(1)}, f32[1,1,16]{2,1,0:T(1,128)S(1)}, u32[]{:S(2)}, u32[]{:S(2)}) collective-permute-start(f32[1,1,16]{2,1,0:T(1,128)S(1)} %divide_add_fusion.8), channel_id=1, source_target_pairs={{0,32},{32,64},{64,96},{96,128},{128,160},{160,192},{192,224},{224... | collective-permute-start | bytes 200 | tf_op jit(solution)/shard_map/ppermute | solution.py:19
  248.6 5.9 %collective-permute-start.52 = (f32[1,3,18]{2,1,0:T(4,128)S(1)}, f32[1,3,18]{2,1,0:T(4,128)S(1)}, u32[]{:S(2)}, u32[]{:S(2)}) collective-permute-start(f32[1,3,18]{2,1,0:T(4,128)S(1)} %pad_maximum_fusion.289), channel_id=1, source_target_pairs={{1,0},{2,1},{3,2},{5,4},{6,5},{7,6},{9,8},{10,9},{11,10},{13,12},{... | collective-permute-start | bytes 656 | tf_op jit(solution)/shard_map/ppermute | solution.py:22
  249.8 5.3 collective-permute-start.53
  255.2 7.4 %collective-permute-start.54 = (f32[1,1,16]{2,1,0:T(1,128)S(1)}, f32[1,1,16]{2,1,0:T(1,128)S(1)}, u32[]{:S(2)}, u32[]{:S(2)}) collective-permute-start(f32[1,1,16]{2,1,0:T(1,128)S(1)} %divide_add_fusion.7), channel_id=1, source_target_pairs={{0,32},{32,64},{64,96},{96,128},{128,160},{160,192},{192,224},{224... | collective-permute-start | bytes 200 | tf_op jit(solution)/shard_map/ppermute | solution.py:19
  272.8 5.9 %collective-permute-start.58 = (f32[1,3,18]{2,1,0:T(4,128)S(1)}, f32[1,3,18]{2,1,0:T(4,128)S(1)}, u32[]{:S(2)}, u32[]{:S(2)}) collective-permute-start(f32[1,3,18]{2,1,0:T(4,128)S(1)} %pad_maximum_fusion.292), channel_id=1, source_target_pairs={{1,0},{2,1},{3,2},{5,4},{6,5},{7,6},{9,8},{10,9},{11,10},{13,12},{... | collective-permute-start | bytes 656 | tf_op jit(solution)/shard_map/ppermute | solution.py:22
  274.1 5.3 collective-permute-start.59
  279.5 7.4 %collective-permute-start.60 = (f32[1,1,16]{2,1,0:T(1,128)S(1)}, f32[1,1,16]{2,1,0:T(1,128)S(1)}, u32[]{:S(2)}, u32[]{:S(2)}) collective-permute-start(f32[1,1,16]{2,1,0:T(1,128)S(1)} %divide_add_fusion.6), channel_id=1, source_target_pairs={{0,32},{32,64},{64,96},{96,128},{128,160},{160,192},{192,224},{224... | collective-permute-start | bytes 200 | tf_op jit(solution)/shard_map/ppermute | solution.py:19
  297.1 5.9 %collective-permute-start.64 = (f32[1,3,18]{2,1,0:T(4,128)S(1)}, f32[1,3,18]{2,1,0:T(4,128)S(1)}, u32[]{:S(2)}, u32[]{:S(2)}) collective-permute-start(f32[1,3,18]{2,1,0:T(4,128)S(1)} %pad_maximum_fusion.295), channel_id=1, source_target_pairs={{1,0},{2,1},{3,2},{5,4},{6,5},{7,6},{9,8},{10,9},{11,10},{13,12},{... | collective-permute-start | bytes 656 | tf_op jit(solution)/shard_map/ppermute | solution.py:22
  298.4 5.3 collective-permute-start.65
  303.8 7.4 %collective-permute-start.66 = (f32[1,1,16]{2,1,0:T(1,128)S(1)}, f32[1,1,16]{2,1,0:T(1,128)S(1)}, u32[]{:S(2)}, u32[]{:S(2)}) collective-permute-start(f32[1,1,16]{2,1,0:T(1,128)S(1)} %divide_add_fusion.5), channel_id=1, source_target_pairs={{0,32},{32,64},{64,96},{96,128},{128,160},{160,192},{192,224},{224... | collective-permute-start | bytes 200 | tf_op jit(solution)/shard_map/ppermute | solution.py:19
  321.4 5.9 %collective-permute-start.70 = (f32[1,3,18]{2,1,0:T(4,128)S(1)}, f32[1,3,18]{2,1,0:T(4,128)S(1)}, u32[]{:S(2)}, u32[]{:S(2)}) collective-permute-start(f32[1,3,18]{2,1,0:T(4,128)S(1)} %pad_maximum_fusion.298), channel_id=1, source_target_pairs={{1,0},{2,1},{3,2},{5,4},{6,5},{7,6},{9,8},{10,9},{11,10},{13,12},{... | collective-permute-start | bytes 656 | tf_op jit(solution)/shard_map/ppermute | solution.py:22
  322.7 5.3 collective-permute-start.71
  328.1 7.4 %collective-permute-start.72 = (f32[1,1,16]{2,1,0:T(1,128)S(1)}, f32[1,1,16]{2,1,0:T(1,128)S(1)}, u32[]{:S(2)}, u32[]{:S(2)}) collective-permute-start(f32[1,1,16]{2,1,0:T(1,128)S(1)} %divide_add_fusion.4), channel_id=1, source_target_pairs={{0,32},{32,64},{64,96},{96,128},{128,160},{160,192},{192,224},{224... | collective-permute-start | bytes 200 | tf_op jit(solution)/shard_map/ppermute | solution.py:19
  345.7 5.9 %collective-permute-start.76 = (f32[1,3,18]{2,1,0:T(4,128)S(1)}, f32[1,3,18]{2,1,0:T(4,128)S(1)}, u32[]{:S(2)}, u32[]{:S(2)}) collective-permute-start(f32[1,3,18]{2,1,0:T(4,128)S(1)} %pad_maximum_fusion.301), channel_id=1, source_target_pairs={{1,0},{2,1},{3,2},{5,4},{6,5},{7,6},{9,8},{10,9},{11,10},{13,12},{... | collective-permute-start | bytes 656 | tf_op jit(solution)/shard_map/ppermute | solution.py:22
  347.0 5.3 collective-permute-start.77
  352.4 7.4 %collective-permute-start.78 = (f32[1,1,16]{2,1,0:T(1,128)S(1)}, f32[1,1,16]{2,1,0:T(1,128)S(1)}, u32[]{:S(2)}, u32[]{:S(2)}) collective-permute-start(f32[1,1,16]{2,1,0:T(1,128)S(1)} %divide_add_fusion.3), channel_id=1, source_target_pairs={{0,32},{32,64},{64,96},{96,128},{128,160},{160,192},{192,224},{224... | collective-permute-start | bytes 200 | tf_op jit(solution)/shard_map/ppermute | solution.py:19
  370.1 5.9 %collective-permute-start.82 = (f32[1,3,18]{2,1,0:T(4,128)S(1)}, f32[1,3,18]{2,1,0:T(4,128)S(1)}, u32[]{:S(2)}, u32[]{:S(2)}) collective-permute-start(f32[1,3,18]{2,1,0:T(4,128)S(1)} %pad_maximum_fusion.304), channel_id=1, source_target_pairs={{1,0},{2,1},{3,2},{5,4},{6,5},{7,6},{9,8},{10,9},{11,10},{13,12},{... | collective-permute-start | bytes 656 | tf_op jit(solution)/shard_map/ppermute | solution.py:22
  371.3 5.3 collective-permute-start.83
  376.9 7.4 %collective-permute-start.84 = (f32[2,1,32]{2,1,0:T(1,128)S(1)}, f32[2,1,32]{2,1,0:T(1,128)S(1)}, u32[]{:S(2)}, u32[]{:S(2)}) collective-permute-start(f32[2,1,32]{2,1,0:T(1,128)S(1)} %get-tuple-element.93), channel_id=1, source_target_pairs={{0,32},{32,64},{64,96},{96,128},{128,160},{160,192},{192,224},{224... | collective-permute-start | bytes 776 | tf_op jit(solution)/shard_map/ppermute | solution.py:19
  394.6 5.8 %collective-permute-start.88 = (f32[1,4,34]{2,1,0:T(4,128)S(1)}, f32[1,4,34]{2,1,0:T(4,128)S(1)}, u32[]{:S(2)}, u32[]{:S(2)}) collective-permute-start(f32[1,4,34]{2,1,0:T(4,128)S(1)} %get-tuple-element.79), channel_id=1, source_target_pairs={{1,0},{2,1},{3,2},{5,4},{6,5},{7,6},{9,8},{10,9},{11,10},{13,12},{... | collective-permute-start | bytes 1640 | tf_op jit(solution)/shard_map/ppermute | solution.py:22
  395.9 5.3 collective-permute-start.89
  401.3 7.4 %collective-permute-start.90 = (f32[2,1,32]{2,1,0:T(1,128)S(1)}, f32[2,1,32]{2,1,0:T(1,128)S(1)}, u32[]{:S(2)}, u32[]{:S(2)}) collective-permute-start(f32[2,1,32]{2,1,0:T(1,128)S(1)} %get-tuple-element.91), channel_id=1, source_target_pairs={{0,32},{32,64},{64,96},{96,128},{128,160},{160,192},{192,224},{224... | collective-permute-start | bytes 776 | tf_op jit(solution)/shard_map/ppermute | solution.py:19
  419.0 5.8 %collective-permute-start.94 = (f32[1,4,34]{2,1,0:T(4,128)S(1)}, f32[1,4,34]{2,1,0:T(4,128)S(1)}, u32[]{:S(2)}, u32[]{:S(2)}) collective-permute-start(f32[1,4,34]{2,1,0:T(4,128)S(1)} %get-tuple-element.75), channel_id=1, source_target_pairs={{1,0},{2,1},{3,2},{5,4},{6,5},{7,6},{9,8},{10,9},{11,10},{13,12},{... | collective-permute-start | bytes 1640 | tf_op jit(solution)/shard_map/ppermute | solution.py:22
  420.3 5.3 collective-permute-start.95
  425.9 7.4 %collective-permute-start.96 = (f32[4,1,64]{2,1,0:T(1,128)S(1)}, f32[4,1,64]{2,1,0:T(1,128)S(1)}, u32[]{:S(2)}, u32[]{:S(2)}) collective-permute-start(f32[4,1,64]{2,1,0:T(1,128)S(1)} %get-tuple-element.69), channel_id=1, source_target_pairs={{0,32},{32,64},{64,96},{96,128},{128,160},{160,192},{192,224},{224... | collective-permute-start | bytes 3080 | tf_op jit(solution)/shard_map/ppermute | solution.py:19
  443.8 5.8 %collective-permute-start.100 = (f32[1,6,66]{2,1,0:T(8,128)S(1)}, f32[1,6,66]{2,1,0:T(8,128)S(1)}, u32[]{:S(2)}, u32[]{:S(2)}) collective-permute-start(f32[1,6,66]{2,1,0:T(8,128)S(1)} %get-tuple-element.45), channel_id=1, source_target_pairs={{1,0},{2,1},{3,2},{5,4},{6,5},{7,6},{9,8},{10,9},{11,10},{13,12},{... | collective-permute-start | bytes 4760 | tf_op jit(solution)/shard_map/ppermute | solution.py:22
  445.1 5.3 collective-permute-start.101
  450.5 7.4 %collective-permute-start.102 = (f32[4,1,64]{2,1,0:T(1,128)S(1)}, f32[4,1,64]{2,1,0:T(1,128)S(1)}, u32[]{:S(2)}, u32[]{:S(2)}) collective-permute-start(f32[4,1,64]{2,1,0:T(1,128)S(1)} %get-tuple-element.67), channel_id=1, source_target_pairs={{0,32},{32,64},{64,96},{96,128},{128,160},{160,192},{192,224},{224... | collective-permute-start | bytes 3080 | tf_op jit(solution)/shard_map/ppermute | solution.py:19
  468.4 5.8 %collective-permute-start.106 = (f32[1,6,66]{2,1,0:T(8,128)S(1)}, f32[1,6,66]{2,1,0:T(8,128)S(1)}, u32[]{:S(2)}, u32[]{:S(2)}) collective-permute-start(f32[1,6,66]{2,1,0:T(8,128)S(1)} %get-tuple-element.43), channel_id=1, source_target_pairs={{1,0},{2,1},{3,2},{5,4},{6,5},{7,6},{9,8},{10,9},{11,10},{13,12},{... | collective-permute-start | bytes 4760 | tf_op jit(solution)/shard_map/ppermute | solution.py:22
  469.7 5.3 collective-permute-start.107
  476.7 7.4 %collective-permute-start.108 = (f32[8,1,128]{2,1,0:T(1,128)S(1)}, f32[8,1,128]{2,1,0:T(1,128)S(1)}, u32[]{:S(2)}, u32[]{:S(2)}) collective-permute-start(f32[8,1,128]{2,1,0:T(1,128)S(1)} %get-tuple-element.53), channel_id=1, source_target_pairs={{0,32},{32,64},{64,96},{96,128},{128,160},{160,192},{192,224},{224... | collective-permute-start | bytes 12296 | tf_op jit(solution)/shard_map/ppermute | solution.py:19
  495.1 5.8 %collective-permute-start.112 = (f32[1,10,130]{2,1,0:T(8,128)S(1)}, f32[1,10,130]{2,1,0:T(8,128)S(1)}, u32[]{:S(2)}, u32[]{:S(2)}) collective-permute-start(f32[1,10,130]{2,1,0:T(8,128)S(1)} %get-tuple-element.29), channel_id=1, source_target_pairs={{1,0},{2,1},{3,2},{5,4},{6,5},{7,6},{9,8},{10,9},{11,10},{13,12},{... | collective-permute-start | bytes 15608 | tf_op jit(solution)/shard_map/ppermute | solution.py:22
  496.4 5.4 %collective-permute-start.113 = (f32[1,10,130]{2,1,0:T(8,128)S(1)}, f32[1,10,130]{2,1,0:T(8,128)S(1)}, u32[]{:S(2)}, u32[]{:S(2)}) collective-permute-start(f32[1,10,130]{2,1,0:T(8,128)S(1)} %get-tuple-element.30), channel_id=1, source_target_pairs={{0,1},{1,2},{2,3},{4,5},{5,6},{6,7},{8,9},{9,10},{10,11},{12,13},{... | collective-permute-start | bytes 15608 | tf_op jit(solution)/shard_map/ppermute | solution.py:19
  502.0 7.4 %collective-permute-start.114 = (f32[8,1,128]{2,1,0:T(1,128)S(1)}, f32[8,1,128]{2,1,0:T(1,128)S(1)}, u32[]{:S(2)}, u32[]{:S(2)}) collective-permute-start(f32[8,1,128]{2,1,0:T(1,128)S(1)} %get-tuple-element.51), channel_id=1, source_target_pairs={{0,32},{32,64},{64,96},{96,128},{128,160},{160,192},{192,224},{224... | collective-permute-start | bytes 12296 | tf_op jit(solution)/shard_map/ppermute | solution.py:19
  520.4 6.0 %collective-permute-start.118 = (f32[1,10,130]{2,1,0:T(8,128)S(1)}, f32[1,10,130]{2,1,0:T(8,128)S(1)}, u32[]{:S(2)}, u32[]{:S(2)}) collective-permute-start(f32[1,10,130]{2,1,0:T(8,128)S(1)} %get-tuple-element.27), channel_id=1, source_target_pairs={{1,0},{2,1},{3,2},{5,4},{6,5},{7,6},{9,8},{10,9},{11,10},{13,12},{... | collective-permute-start | bytes 15608 | tf_op jit(solution)/shard_map/ppermute | solution.py:22
  521.7 5.5 %collective-permute-start.119 = (f32[1,10,130]{2,1,0:T(8,128)S(1)}, f32[1,10,130]{2,1,0:T(8,128)S(1)}, u32[]{:S(2)}, u32[]{:S(2)}) collective-permute-start(f32[1,10,130]{2,1,0:T(8,128)S(1)} %get-tuple-element.28), channel_id=1, source_target_pairs={{0,1},{1,2},{2,3},{4,5},{5,6},{6,7},{8,9},{9,10},{10,11},{12,13},{... | collective-permute-start | bytes 15608 | tf_op jit(solution)/shard_map/ppermute | solution.py:19
  (62 other events, 281.9 us)
where the time goes:
time: 537 us; the launch traced here: 528 us
  starting transfers between devices  350 us (65%)
  waiting for transfers between devices  130 us (24%)
  local copies, waits for them, and re-layouts  30.4 us (6%)
  other arithmetic  15.5 us (3%)
    ppermute x60, starting transfers between devices, padded_2(): lax.ppermute(lax.slice_in_dim(block, block.shape[dim] - width, None, axis...  257 us
    ppermute x60, waiting for transfers between devices, padded_2(): lax.ppermute(lax.slice_in_dim(block, 0, width, axis=dim), axis, backward)  117 us
    ppermute x60, starting transfers between devices, padded_2(): lax.ppermute(lax.slice_in_dim(block, 0, width, axis=dim), axis, backward)  92.9 us
    ppermute x60, waiting for transfers between devices, padded_2(): lax.ppermute(lax.slice_in_dim(block, block.shape[dim] - width, None, axis...  12.8 us
    reshape x16, local copies, waits for them, and re-layouts, coarse_faces(): blocks = values.reshape(dims[0] // 2, 2, dims[1] // 2, 2, dims[2] // 2, 2)  11.8 us
  transfers between devices with their start and end apart: 120, of which 59 were waited for; matrix products, arithmetic and copies ran while one was open for 6% of the time, Pallas kernels for 0%

commit v1 on v0

v1 whole, which is shorter than its diff:
```python
import jax
import jax.numpy as jnp
from jax import lax
from jax.experimental import pallas as pl
from jax.experimental.pallas import tpu as pltpu
from jax.sharding import PartitionSpec as P

MESH = pl.DeviceIdType.MESH
SIZES = (("gz", 4), ("gx", 16), ("gy", 8))
F32 = jnp.float32
RELAX = 0.7
KEEP = 1.0 - RELAX

ZX = [(k, a) for k in range(4) for a in (0, 1, -1) if (k, a) != (0, 0)]


def at(offset):
    return {
        name: lax.rem(lax.axis_index(name) + (step + size), size)
        for (name, size), step in zip(SIZES, offset)
    }


class Net:
    def __init__(self, send_sems, recv_sems):
        self.send_sems, self.recv_sems, self.copies = send_sems, recv_sems, []

    def send(self, src, dst, offset):
        index = len(self.copies)
        copy = pltpu.make_async_remote_copy(
            src_ref=src,
            dst_ref=dst,
            send_sem=self.send_sems.at[index],
            recv_sem=self.recv_sems.at[index],
            device_id=at(offset),
            device_id_type=MESH,
        )
        copy.start()
        self.copies.append(copy)
        return copy


def wait(copies):
    for copy in copies:
        copy.wait_recv()


def iota(shape, dim):
    return lax.broadcasted_iota(jnp.int32, shape, dim)


def mat(rows, cols, where):
    return jnp.where(where(iota((rows, cols), 0), iota((rows, cols), 1)), 1.0, 0.0).astype(F32)


def dot(a, b):
    return jnp.dot(a, b, preferred_element_type=F32, precision=lax.Precision.HIGHEST)


def roll(x, shift, axis):
    size = x.shape[axis]
    shift = shift % size
    return pltpu.roll(x, shift, axis) if shift else x


def low_lanes(i, parity):
    if parity is None:
        return i >= 0
    return (i & 1) == parity


PICKS = ((1, None, None), (0, None, None), (None, 1, None), (None, 0, None), (None, None, 1), (None, None, 0), (None, None, None))


def kernel(
    src_ref, r_ref, k_ref, v_ref, f_ref, out_ref,
    e0a, e0z, e0y, xb0, zlo, zhi, ylo, yhi,
    ea, ex, ey, exy, pk, pkr,
    cu, d0, va, vx, vy,
    wa, wx, wpk, wpkr,
    ys, ylr, yhr, c1, c2, c3,
    b1c, b1r, b1l, b1h, b1, v1p, v1q,
    b2c, b2r, b2l, b2h, b2, v2p, v2q,
    b3, go_a, go_b, ssem, rsem,
):
    net = Net(ssem, rsem)
    send = net.send
    gz, gx, gy = lax.axis_index("gz"), lax.axis_index("gx"), lax.axis_index("gy")
    sx, ly = iota((8, 128), 0), iota((8, 128), 1)

    barrier = pltpu.get_barrier_semaphore()
    greeted = [(1, 0, 0), (2, 0, 0), (3, 0, 0), (0, 1, 0), (0, -1, 0), (0, 0, 1), (0, 0, -1)]
    for offset in greeted:
        pl.semaphore_signal(barrier, inc=1, device_id=at(offset), device_id_type=MESH)

    e0a[0] = k_ref[1]
    e0a[1] = v_ref[1]
    e0a[2] = f_ref[1].astype(F32)
    e0z[0] = k_ref[0, 7]
    e0z[1] = v_ref[0, 7]
    e0z[2] = f_ref[0, 7].astype(F32)
    e0z[3] = k_ref[0, 0]
    e0z[4] = v_ref[0, 0]
    packed = jnp.zeros((8, 128), F32)
    for f, ref in enumerate((k_ref, v_ref, f_ref)):
        for z in range(8):
            start = 16 * f + 2 * z
            moved = roll(ref[2, z].astype(F32), start + 1, 1)
            packed = jnp.where((ly >= start) & (ly < start + 2), moved, packed)
    e0y[...] = packed
    pl.semaphore_wait(barrier, len(greeted))
    e0 = [
        send(e0a.at[:, :, pl.ds(7, 1), :], xb0.at[:, :, pl.ds(7, 1), :], (0, 1, 0)),
        send(e0a.at[pl.ds(0, 2), :, pl.ds(0, 1), :], xb0.at[pl.ds(0, 2), :, pl.ds(0, 1), :], (0, -1, 0)),
        send(e0z.at[pl.ds(0, 3)], zlo, (1, 0, 0)),
        send(e0z.at[pl.ds(3, 2)], zhi, (-1, 0, 0)),
        send(e0y, ylo, (0, 0, 1)),
        send(e0y, yhi, (0, 0, -1)),
    ]

    def xprev(a, b):
        return roll(jnp.where(sx == 7, b, a), 1, 0)

    def xnext(a, b):
        return roll(jnp.where(sx == 0, b, a), -1, 0)

    def yprev(a, b):
        return roll(jnp.where(ly == 127, b, a), 1, 1)

    def ynext(a, b):
        return roll(jnp.where(ly == 0, b, a), -1, 1)

    wait(e0)
    for a in (2, -2):
        pl.semaphore_signal(go_a, inc=1, device_id=at((0, a, 0)), device_id_type=MESH)

    both0 = jnp.where((ly & 1) == 0, ylo[...], yhi[...])
    pack = jnp.zeros((8, 128), F32)
    for z in range(8):
        k, v = [k_ref[d, z] for d in range(3)], [v_ref[d, z] for d in range(3)]
        f = [f_ref[d, z].astype(F32) for d in range(3)]
        side = [roll(both0, -(16 * q + 2 * z + 1), 1) for q in range(3)]
        kn = [
            k_ref[0, z + 1] if z < 7 else zhi[0],
            xnext(k[1], xb0[0, z]),
            ynext(k[2], side[0]),
        ]
        vn = [
            v_ref[0, z + 1] if z < 7 else zhi[1],
            xnext(v[1], xb0[1, z]),
            ynext(v[2], side[1]),
        ]
        kp = [
            k_ref[0, z - 1] if z else zlo[0],
            xprev(k[1], xb0[0, z]),
            yprev(k[2], side[0]),
        ]
        vp = [
            v_ref[0, z - 1] if z else zlo[1],
            xprev(v[1], xb0[1, z]),
            yprev(v[2], side[1]),
        ]
        fp = [
            f_ref[0, z - 1].astype(F32) if z else zlo[2],
            xprev(f[1], xb0[2, z]),
            yprev(f[2], side[2]),
        ]
        last = [
            (gz == 3) if z == 7 else None,
            (sx == 7) & (gx == 15),
            (ly == 127) & (gy == 7),
        ]
        first = [
            (gz == 0) if z == 0 else None,
            (sx == 0) & (gx == 0),
            (ly == 0) & (gy == 0),
        ]
        terms = []
        for d in range(3):
            up = 0.5 * (k[d] + kn[d]) + f[d] * (0.5 * (v[d] + vn[d]))
            down = 0.5 * (kp[d] + k[d]) + (1.0 - fp[d]) * (0.5 * (vp[d] + v[d]))
            if last[d] is not None:
                up = jnp.where(last[d], 0.0, up)
            if first[d] is not None:
                down = jnp.where(first[d], 0.0, down)
            terms += [up, down]
        rate = r_ref[z]
        diag = rate
        for term in terms:
            diag = diag + term
        scale = RELAX / diag
        d0[z] = diag * (1.0 / RELAX)
        for q in range(6):
            cu[q, z] = terms[q]
            scaled = terms[q] * scale
            ea[1 + q, 2 + z] = scaled
            start = 32 + 16 * q + 2 * z
            pack = jnp.where((ly >= start) & (ly < start + 2), roll(scaled, start + 1, 1), pack)
        begun = src_ref[z] * scale
        ea[0, 2 + z] = begun
        pack = jnp.where((ly >= 4 * z) & (ly < 4 * z + 4), roll(begun, 4 * z + 2, 1), pack)
    pk[...] = pack

    diagonal_y = [(0, 0, 1), (0, 0, -1)] + [(s, 0, t) for s in (1, -1) for t in (1, -1)] + [(0, s, t) for s in (1, -1) for t in (1, -1)]

    def rim(a, x, p, pr):
        copies = []
        for s in (1, -1):
            mine, theirs = (8, 0) if s == 1 else (2, 10)
            copies.append(send(a.at[pl.ds(mine, 2)], a.at[pl.ds(theirs, 2)], (s, 0, 0)))
            row = 6 if s == 1 else 0
            copies.append(send(a.at[pl.ds(2, 8), pl.ds(row, 2)], x.at[pl.ds(1, 8), pl.ds(row, 2)], (0, s, 0)))
        for i, offset in enumerate(diagonal_y):
            copies.append(send(p, pr.at[i], offset))
        for s in (1, -1):
            for t in (1, -1):
                plane, row = (9 if s == 1 else 2), (7 if t == 1 else 0)
                copies.append(
                    send(a.at[pl.ds(plane, 1), pl.ds(row, 1)], x.at[pl.ds(0 if s == 1 else 9, 1), pl.ds(row, 1)], (s, t, 0))
                )
        return copies

    r1 = []
    for s in (1, -1):
        mine, theirs, row = (9, 1, 7) if s == 1 else (2, 10, 0)
        r1.append(send(ea.at[pl.ds(1, 6), pl.ds(mine, 1)], ea.at[pl.ds(1, 6), pl.ds(theirs, 1)], (s, 0, 0)))
        r1.append(
            send(ea.at[pl.ds(1, 6), pl.ds(2, 8), pl.ds(row, 1)], ex.at[pl.ds(1, 6), pl.ds(1, 8), pl.ds(row, 1)], (0, s, 0))
        )
    r1 += rim(ea.at[0], ex.at[0], pk, pkr)

    own1 = (iota((16, 128), 1) >= 32) & (iota((16, 128), 1) < 96)

    def scaled_terms(fields, inside):
        diag = fields[6]
        for q in range(6):
            diag = diag + fields[q]
        diag = jnp.where(inside, diag, 1.0)
        scale = jnp.where(inside, RELAX / diag, 0.0)
        return [fields[q] * scale for q in range(6)] + [jnp.where(inside, diag * (1.0 / RELAX), 0.0)]

    def pairs(q, a, b):
        pick = PICKS[q][0]
        return a + b if pick is None else (b if pick else a)

    def lanes01(pick):
        return mat(128, 128, lambda i, j: (j == 32 + (i >> 1)) & low_lanes(i, pick))

    def lanes12(pick):
        return mat(128, 128, lambda i, j: (j == 16 + (i >> 1)) & (i >= 32) & (i < 96) & low_lanes(i, pick))

    def lanes23(pick):
        return mat(128, 128, lambda i, j: (j == (i >> 1)) & (i >= 32) & (i < 64) & low_lanes(i, pick))

    def rows01(pick):
        return mat(16, 32, lambda i, j: ((j >> 3) == (i & 3)) & (((j & 7) >> 1) == (i >> 2)) & low_lanes(j, pick))

    def rows12(pz, px):
        return mat(
            8, 16,
            lambda i, j: ((j >> 3) == (i >> 1)) & (((j & 3) >> 1) == (i & 1)) & low_lanes(j, pz) & low_lanes(j >> 2, px),
        )

    def rows23(pz, px):
        return mat(8, 8, lambda i, j: (i == 0) & (j < 4) & low_lanes(j, pz) & low_lanes(j >> 1, px))

    level1 = []
    for q in range(7):
        planes = [pairs(q, (cu[q, 2 * z] if q < 6 else r_ref[2 * z]), (cu[q, 2 * z + 1] if q < 6 else r_ref[2 * z + 1])) for z in range(4)]
        stacked = jnp.concatenate(planes, axis=0)
        level1.append(dot(dot(rows01(PICKS[q][1]), stacked), lanes01(PICKS[q][2])))
    level2 = [dot(dot(rows12(PICKS[q][0], PICKS[q][1]), level1[q]), lanes12(PICKS[q][2])) for q in range(7)]
    level3 = [dot(dot(rows23(PICKS[q][0], PICKS[q][1]), level2[q]), lanes23(PICKS[q][2])) for q in range(7)]
    inside2 = (ly >= 32) & (ly < 64) & (sx < 4)
    inside3 = (ly >= 16) & (ly < 32) & (sx < 1)
    scaled1 = scaled_terms(level1, own1)
    scaled2 = scaled_terms(level2, inside2)
    scaled3 = scaled_terms(level3, inside3)
    for q in range(7):
        ys[pl.ds(16 * q, 16), :] = roll(scaled1[q], 64, 1)
        ys[pl.ds(112 + 8 * q, 8), :] = roll(scaled2[q], 32, 1) + roll(scaled2[q], -32, 1)
        ys[pl.ds(168 + 8 * q, 8), :] = roll(scaled3[q], 16, 1) + roll(scaled3[q], -16, 1)
    stage_y = [send(ys, ylr, (0, 0, 1)), send(ys, yhr, (0, 0, -1))]

    wait(stage_y)
    lane16 = iota((16, 128), 1)
    for q in range(7):
        part = pl.ds(16 * q, 16)
        merged = jnp.where(lane16 < 32, ylr[part, :], jnp.where(lane16 >= 96, yhr[part, :], scaled1[q]))
        for x in range(4):
            c1[q, 4 + x, 0:4, :] = merged[4 * x : 4 * x + 4]
        part = pl.ds(112 + 8 * q, 8)
        merged = jnp.where(ly < 32, ylr[part, :], jnp.where(ly >= 64, yhr[part, :], scaled2[q]))
        for x in range(2):
            c2[q, 6 + x, 0:2, :] = merged[2 * x : 2 * x + 2]
        part = pl.ds(168 + 8 * q, 8)
        merged = jnp.where(ly < 16, ylr[part, :], jnp.where(ly >= 32, yhr[part, :], scaled3[q]))
        c3[q, 0, 0:1, :] = merged[0:1]

    def zslot(k):
        return (4 - k) % 4

    def xplace(own, per, a):
        return own - per * a

    c1_copies = [
        send(c1.at[:, pl.ds(4, 4), pl.ds(0, 4)], c1.at[:, pl.ds(xplace(4, 4, a), 4), pl.ds(4 * zslot(k), 4)], (k, a, 0))
        for k, a in ZX
    ]
    z_copies = []
    for k in (1, 2, 3):
        z_copies.append(send(c2.at[:, pl.ds(6, 2), pl.ds(0, 2)], c2.at[:, pl.ds(6, 2), pl.ds(2 * zslot(k), 2)], (k, 0, 0)))
        z_copies.append(send(c3.at[:, pl.ds(0, 1), pl.ds(0, 1)], c3.at[:, pl.ds(0, 1), pl.ds(zslot(k), 1)], (k, 0, 0)))

    wait(r1)
    pl.semaphore_wait(go_a, 2)
    for a in (4, -4):
        pl.semaphore_signal(go_b, inc=1, device_id=at((0, a, 0)), device_id_type=MESH)

    def unpack(pr, y, xy):
        from_low = (ly & jnp.where(ly < 32, 2, 1)) == 0

        def both(low, high):
            return jnp.where(from_low, pr[low], pr[high])

        beside = both(0, 1)
        for z in range(8):
            y[1 + z] = roll(beside, -(4 * z + 2), 1)
        y[0] = roll(both(2, 3), -30, 1)
        y[9] = roll(both(4, 5), -2, 1)
        across = jnp.where(sx < 4, both(8, 9), both(6, 7))
        for z in range(8):
            xy[z] = roll(across, -(4 * z + 2), 1)
        return beside

    beside = unpack(pkr, ey.at[0], exy)
    for q in range(6):
        for z in range(8):
            ey[1 + q, 1 + z] = roll(beside, -(32 + 16 * q + 2 * z + 1), 1)

    def sweep(here, zp, zn, xp, xn, yp, yn, rhs, s):
        total = KEEP * here + rhs
        total = total + s[0] * zn + s[1] * zp
        total = total + s[2] * xn + s[3] * xp
        return total + s[4] * yn + s[5] * yp

    def sweep_a(a, x, y, p, outer):
        here = a[p]
        bx, by = x[p - outer], y[p - outer]
        return sweep(
            here, a[p - 1], a[p + 1], xprev(here, bx), xnext(here, bx), yprev(here, by), ynext(here, by),
            ea[0, p], [ea[1 + q, p] for q in range(6)],
        )

    def rim_sweep(a, x, y, xy):
        for p in range(1, 11):
            va[p] = sweep_a(a, x, y, p, 1)
        for z in range(8):
            here = x[1 + z]
            ba, bxy = a[2 + z], xy[z]
            vx[z] = sweep(
                here, x[z], x[2 + z], xprev(here, ba), xnext(here, ba), yprev(here, bxy), ynext(here, bxy),
                ex[0, 1 + z], [ex[1 + q, 1 + z] for q in range(6)],
            )
            here = y[1 + z]
            vy[z] = sweep(
                here, y[z], y[2 + z], xprev(here, bxy), xnext(here, bxy), yprev(here, ba), ynext(here, ba),
                ey[0, 1 + z], [ey[1 + q, 1 + z] for q in range(6)],
            )

    rim_sweep(ea.at[0], ex.at[0], ey.at[0], exy)
    planes = []
    for z in range(4):
        two = [(sweep_a(va, vx, vy, 2 + p, 2) - va[2 + p]) * d0[p] for p in (2 * z, 2 * z + 1)]
        planes.append(two[0] + two[1])
    rhs1 = dot(dot(rows01(None), jnp.concatenate(planes, axis=0)), lanes01(None))
    d1_own = jnp.concatenate([c1[6, 4 + x, 0:4, :] for x in range(4)], axis=0)
    rhs1 = jnp.where(own1, rhs1 / jnp.where(own1, d1_own, 1.0), 0.0)
    turned = roll(rhs1, 64, 1)
    for x in range(4):
        b1c[4 + x, 0:4, :] = rhs1[4 * x : 4 * x + 4]
        b1r[x, 0:4, :] = turned[4 * x : 4 * x + 4]

    r2 = []
    for k, a in ZX:
        there = (pl.ds(xplace(4, 4, a), 4), pl.ds(4 * zslot(k), 4))
        r2.append(send(b1c.at[pl.ds(4, 4), pl.ds(0, 4)], b1c.at[there], (k, a, 0)))
    for k, a in [(0, 0)] + ZX:
        there = (pl.ds(xplace(4, 4, a), 4), pl.ds(4 * zslot(k), 4))
        r2.append(send(b1r.at[:, pl.ds(0, 4)], b1l.at[there], (k, a, 1)))
        r2.append(send(b1r.at[:, pl.ds(0, 4)], b1h.at[there], (k, a, -1)))

    pack = jnp.zeros((8, 128), F32)
    for z in range(8):
        plane = va[2 + z]
        wa[2 + z] = plane
        pack = jnp.where((ly >= 4 * z) & (ly < 4 * z + 4), roll(plane, 4 * z + 2, 1), pack)
    wpk[...] = pack
    up0 = rim(wa, wx, wpk, wpkr)

    wait(z_copies)
    c2_copies = [
        send(c2.at[:, pl.ds(6, 2)], c2.at[:, pl.ds(xplace(6, 2, a), 2)], (0, a, 0)) for a in (1, -1, 2, -2, 3, -3)
    ]

    def sweep_l(v, b, c, x):
        here = v[x]
        return sweep(
            here, roll(here, 1, 0), roll(here, -1, 0), v[x - 1], v[x + 1], roll(here, 1, 1), roll(here, -1, 1),
            b[x], [c[q, x] for q in range(6)],
        )

    wait(c1_copies)
    wait(r2)
    for x in range(12):
        b1[x] = jnp.where(lane16 < 32, b1l[x], jnp.where(lane16 >= 96, b1h[x], b1c[x]))
    for x in range(1, 11):
        v1p[x] = sweep_l(b1, b1, c1, x)
    rows = []
    for x in range(2):
        two = [(sweep_l(v1p, b1, c1, p) - v1p[p]) * c1[6, p] for p in (4 + 2 * x, 5 + 2 * x)]
        rows.append(two[0] + two[1])
    rows = dot(jnp.concatenate(rows, axis=0), lanes12(None))
    halve = mat(8, 16, lambda i, j: (j >> 1) == i)
    for x in range(2):
        inside = (ly >= 32) & (ly < 64)
        rhs2 = dot(halve, rows[16 * x : 16 * x + 16])
        rhs2 = jnp.where(inside, rhs2 / jnp.where(inside, c2[6, 6 + x], 1.0), 0.0)
        b2c[6 + x] = rhs2
        b2r[x] = roll(rhs2, 32, 1) + roll(rhs2, -32, 1)

    r3 = []
    for a in (0, 1, -1, 2, -2, 3, -3):
        there = pl.ds(xplace(6, 2, a), 2)
        if a:
            r3.append(send(b2c.at[pl.ds(6, 2)], b2c.at[there], (0, a, 0)))
        r3.append(send(b2r, b2l.at[there], (0, a, 1)))
        r3.append(send(b2r, b2h.at[there], (0, a, -1)))
    pl.semaphore_wait(go_b, 2)
    c3_copies = [
        send(c3.at[pl.ds(0, 6), pl.ds(0, 1), pl.ds(0, 4)], c3.at[pl.ds(0, 6), pl.ds(16 - a, 1), pl.ds(0, 4)], (0, a, 0))
        for a in range(1, 16)
    ]

    wait(c2_copies)
    wait(r3)
    for x in range(14):
        b2[x] = jnp.where(ly < 32, b2l[x], jnp.where(ly >= 64, b2h[x], b2c[x]))
    for x in range(2, 12):
        v2p[x] = sweep_l(b2, b2, c2, x)
    two = [(sweep_l(v2p, b2, c2, p) - v2p[p]) * c2[6, p] for p in (6, 7)]
    rows = dot(two[0] + two[1], mat(128, 128, lambda i, j: (j == (i >> 1)) & (i < 96)))
    rhs3 = dot(mat(8, 8, lambda i, j: (j >> 1) == (i & 3)), rows)

    def twice(block):
        return jnp.where(sx < 4, block, roll(block, 4, 0))

    inside = ly < 48
    rhs3 = jnp.where(inside, rhs3 / jnp.where(inside, twice(c3[6, 0]), 1.0), 0.0)
    b3[0] = rhs3

    r4 = [send(b3.at[pl.ds(0, 1)], b3.at[pl.ds(16 - a, 1)], (0, a, 0)) for a in range(1, 16)]
    wait(c3_copies)
    terms3 = [[twice(c3[q, x]) for x in range(16)] for q in range(6)]
    wait(r4)
    rhs3 = [b3[x] for x in range(16)]
    here = rhs3
    for _ in range(7):
        here = [
            sweep(
                here[x], roll(here[x], 1, 0), roll(here[x], -1, 0), here[(x + 15) % 16], here[(x + 1) % 16],
                roll(here[x], 1, 1), roll(here[x], -1, 1), rhs3[x], [terms3[q][x] for q in range(6)],
            )
            for x in range(16)
        ]

    wide = dot(mat(8, 8, lambda i, j: j == (i >> 1)), jnp.concatenate([here[(X + 16) % 16] for X in range(-2, 3)], axis=1))
    wide = jnp.concatenate([wide[:, 128 * i : 128 * i + 128] for i in range(5)], axis=0)
    wide = dot(wide, mat(128, 128, lambda i, j: (i == (j >> 1)) & (j < 96)))
    for x in range(2, 12):
        i = (x >> 1) - 1
        v2p[x] = v2p[x] + wide[8 * i : 8 * i + 8]
    for x in range(3, 11):
        v2q[x] = sweep_l(v2p, b2, c2, x)
    ups = [sweep_l(v2q, b2, c2, x) for x in range(4, 10)]

    wide = dot(jnp.concatenate(ups, axis=0), mat(128, 128, lambda i, j: i == 16 + (j >> 1)))
    wide = dot(mat(16, 8, lambda i, j: j == (i >> 1)), jnp.concatenate([wide[8 * i : 8 * i + 8] for i in range(6)], axis=1))
    for x in range(1, 11):
        i = x >> 1
        v1p[x] = v1p[x] + wide[:, 128 * i : 128 * i + 128]
    for x in range(2, 10):
        v1q[x] = sweep_l(v1p, b1, c1, x)
    ups = [sweep_l(v1q, b1, c1, x) for x in range(3, 9)]

    def lanes10(i, j):
        main = (j < 128) & (i == 32 + (j >> 1))
        return main | ((j >= 254) & (i == 31)) | ((j >= 128) & (j < 130) & (i == 96))

    def rows10(i, j):
        xi, zr = j >> 4, j & 15
        main = (i < 96) & (zr == (((i >> 4) + 15) & 15)) & (xi == 1 + ((i & 7) >> 1))
        n = i - 96
        beside = (i >= 96) & (zr == ((((n >> 3) + 31) >> 1) & 15)) & (
            (((n & 7) >= 6) & (xi == 0)) | (((n & 7) < 2) & (xi == 5))
        )
        return main | beside

    wide = dot(jnp.concatenate(ups, axis=0), mat(128, 256, lanes10))
    wide = dot(mat(176, 96, rows10), wide)
    wait(up0)
    low = (ly & 2) == 0
    beside = jnp.where(low, wpkr[0], wpkr[1])
    low_z = jnp.where(low, wpkr[2], wpkr[3])
    high_z = jnp.where(low, wpkr[4], wpkr[5])
    across = jnp.where(sx < 4, jnp.where(low, wpkr[8], wpkr[9]), jnp.where(low, wpkr[6], wpkr[7]))
    a = [wa[p] + wide[8 * p : 8 * p + 8, 0:128] for p in range(12)]
    x = [wx[p] + wide[96 + 8 * p : 104 + 8 * p, 0:128] for p in range(10)]
    y = []
    for p in range(10):
        if p == 0:
            base = roll(low_z, -30, 1)
        elif p == 9:
            base = roll(high_z, -2, 1)
        else:
            base = roll(beside, -(4 * (p - 1) + 2), 1)
        y.append(base + wide[8 * (p + 1) : 8 * (p + 1) + 8, 128:256])
    xy = [roll(across, -(4 * z + 2), 1) + wide[104 + 8 * z : 112 + 8 * z, 128:256] for z in range(8)]
    rim_sweep(a, x, y, xy)
    for z in range(8):
        out_ref[z] = sweep_a(va, vx, vy, 2 + z, 2)
    for copy in net.copies:
        copy.wait_send()


def on_device(source, decay_rate, dispersion, velocity, upwind):
    def vmem(*shape):
        return pltpu.VMEM(shape, F32)

    tile = (8, 128)
    scratch = [
        vmem(3, 8, *tile), vmem(5, *tile), vmem(*tile), vmem(3, 8, *tile), vmem(3, *tile), vmem(2, *tile), vmem(*tile), vmem(*tile),
        vmem(7, 12, *tile), vmem(7, 10, *tile), vmem(7, 10, *tile), vmem(8, *tile), vmem(*tile), vmem(10, *tile),
        vmem(6, 8, *tile), vmem(8, *tile), vmem(12, *tile), vmem(8, *tile), vmem(8, *tile),
        vmem(12, *tile), vmem(10, *tile), vmem(*tile), vmem(10, *tile),
        vmem(224, 128), vmem(224, 128), vmem(224, 128), vmem(7, 12, 16, 128), vmem(7, 14, *tile), vmem(7, 16, *tile),
        vmem(12, 16, 128), vmem(4, *tile), vmem(12, 16, 128), vmem(12, 16, 128), vmem(12, 16, 128), vmem(12, 16, 128), vmem(12, 16, 128),
        vmem(14, *tile), vmem(2, *tile), vmem(14, *tile), vmem(14, *tile), vmem(14, *tile), vmem(14, *tile), vmem(14, *tile),
        vmem(16, *tile),
        pltpu.SemaphoreType.REGULAR, pltpu.SemaphoreType.REGULAR,
        pltpu.SemaphoreType.DMA((160,)), pltpu.SemaphoreType.DMA((160,)),
    ]
    return pl.pallas_call(
        kernel,
        out_shape=jax.ShapeDtypeStruct((8, 8, 128), F32),
        in_specs=[pl.BlockSpec(memory_space=pltpu.VMEM)] * 5,
        out_specs=pl.BlockSpec(memory_space=pltpu.VMEM),
        scratch_shapes=scratch,
        compiler_params=pltpu.CompilerParams(
            collective_id=0, has_side_effects=True, vmem_limit_bytes=32 * 1024 * 1024
        ),
    )(source, decay_rate, dispersion, velocity, upwind)


def solution(mesh):
    field, vector = P("gz", "gx", "gy"), P(None, "gz", "gx", "gy")
    return jax.shard_map(
        on_device, mesh=mesh, in_specs=(field, field, vector, vector, vector), out_specs=field, check_vma=False
    )
```

time: 537 us -> 62.3 us (0.12); the launches traced: 528 us -> 62 us
  starting transfers between devices: 350 us -> 0 us
  waiting for transfers between devices: 130 us -> 0 us
  Pallas kernels: 0 us -> 57.1 us
  local copies, waits for them, and re-layouts: 30.4 us -> 4.81 us
  other arithmetic: 15.5 us -> 0 us
    ppermute x120 -> x0, starting transfers between devices: 350 us -> none  [the longest x60 257 us: padded_2(): lax.ppermute(lax.slice_in_dim(block, block.shape[dim] - width, None, axis...]
    ppermute x120 -> x0, waiting for transfers between devices: 130 us -> none  [the longest x60 117 us: padded_2(): lax.ppermute(lax.slice_in_dim(block, 0, width, axis=dim), axis, backward)]
    pallas_call x0 -> x1, Pallas kernels: none -> 57.1 us  [on_device(): pl.pallas_call(kernel, out_shape=jax.ShapeDtypeStruct((8, 8, 128), F32),...]
    reshape x22 -> x0, local copies, waits for them, and re-layouts: 18.6 us -> none  [the longest x16 11.8 us: coarse_faces(): blocks = values.reshape(dims[0] // 2, 2, dims[1] // 2, 2, dims[2] // 2, 2)]
    add x2 -> x0, local copies, waits for them, and re-layouts: 6.82 us -> none  [the longest x1 3.41 us: face_pair(): 0.5 * (k_prev + k_here) + (1.0 - f_prev) * (0.5 * (v_prev + v_here))]
    reduce_sum x28 -> x0, other arithmetic: 6.17 us -> none  [the longest x18 4.9 us: coarse_faces(): return chosen.sum(axis=(1, 3, 5))]
  transfers between devices with their start and end apart: 120 -> 0, of which waited for: 59 -> 0; matrix products, arithmetic and copies ran while one was open for 6% -> 0% of each run, Pallas kernels for 0% -> 0%
where the time goes in v1:
time: 62.3 us; the launch traced here: 62 us
  Pallas kernels  57.1 us (92%)
  local copies, waits for them, and re-layouts  4.81 us (8%)
    pallas_call x1, Pallas kernels, on_device(): pl.pallas_call(kernel, out_shape=jax.ShapeDtypeStruct((8, 8, 128), F32),...  57.1 us
    unnamed x11, local copies, waits for them, and re-layouts  4.81 us

profile of v1, /device:TPU:1, one launch (start us, length us, event | category | flops | bytes accessed | tf_op | source)
XLA Modules:
  0.0 62.0 jit_solution(11912940202613876202)
XLA Ops:
  0.0 0.0 copy-start
  0.0 0.9 %copy-done = f32[3,8,8,128]{3,2,1,0:T(8,128)S(1)} copy-done((f32[3,8,8,128]{3,2,1,0:T(8,128)S(1)}, f32[3,8,8,128]{3,2,1,0:T(8,128)}, u32[]{:S(2)}) %copy-start) | copy-done | bytes 98328
  0.9 0.0 copy-start.1
  0.9 0.9 %copy-done.1 = f32[3,8,8,128]{3,2,1,0:T(8,128)S(1)} copy-done((f32[3,8,8,128]{3,2,1,0:T(8,128)S(1)}, f32[3,8,8,128]{3,2,1,0:T(8,128)}, u32[]{:S(2)}) %copy-start.1) | copy-done | bytes 98328
  1.8 0.0 copy-start.2
  1.8 0.9 %copy-done.2 = s32[3,8,8,128]{3,2,1,0:T(8,128)S(1)} copy-done((s32[3,8,8,128]{3,2,1,0:T(8,128)S(1)}, s32[3,8,8,128]{3,2,1,0:T(8,128)}, u32[]{:S(2)}) %copy-start.2) | copy-done | bytes 98328
  2.7 0.0 copy-start.3
  2.7 0.8 %copy-done.3 = f32[8,8,128]{2,1,0:T(8,128)S(1)} copy-done((f32[8,8,128]{2,1,0:T(8,128)S(1)}, f32[8,8,128]{2,1,0:T(8,128)}, u32[]{:S(2)}) %copy-start.3) | copy-done | bytes 32792
  3.4 0.0 copy-start.4
  3.4 0.8 %copy-done.4 = f32[8,8,128]{2,1,0:T(8,128)S(1)} copy-done((f32[8,8,128]{2,1,0:T(8,128)S(1)}, f32[8,8,128]{2,1,0:T(8,128)}, u32[]{:S(2)}) %copy-start.4) | copy-done | bytes 32792
  4.2 57.1 %shard_map.55 = f32[8,8,128]{2,1,0:T(8,128)S(1)} custom-call(f32[8,8,128]{2,1,0:T(8,128)S(1)} %copy-done.3, f32[8,8,128]{2,1,0:T(8,128)S(1)} %copy-done.4, f32[3,8,8,128]{3,2,1,0:T(8,128)S(1)} %copy-done, f32[3,8,8,128]{3,2,1,0:T(8,128)S(1)} %copy-done.1, s32[3,8,8,128]{3,2,1,0:T(8,128)S(1)} %copy-done.2), custom_call_target="tpu_custom_call" | custom-call | tf_op jit(solution)/shard_map/pallas_call | solution.py:553
  61.3 0.6 copy.7
Async XLA Ops:
  0.0 0.9 %copy-start = (f32[3,8,8,128]{3,2,1,0:T(8,128)S(1)}, f32[3,8,8,128]{3,2,1,0:T(8,128)}, u32[]{:S(2)}) copy-start(f32[3,8,8,128]{3,2,1,0:T(8,128)} %k_ref.1) | copy-start | bytes 294916
  0.9 0.9 %copy-start.1 = (f32[3,8,8,128]{3,2,1,0:T(8,128)S(1)}, f32[3,8,8,128]{3,2,1,0:T(8,128)}, u32[]{:S(2)}) copy-start(f32[3,8,8,128]{3,2,1,0:T(8,128)} %v_ref.1) | copy-start | bytes 294916
  1.8 0.9 %copy-start.2 = (s32[3,8,8,128]{3,2,1,0:T(8,128)S(1)}, s32[3,8,8,128]{3,2,1,0:T(8,128)}, u32[]{:S(2)}) copy-start(s32[3,8,8,128]{3,2,1,0:T(8,128)} %f_ref.1) | copy-start | bytes 294916
  2.7 0.8 %copy-start.3 = (f32[8,8,128]{2,1,0:T(8,128)S(1)}, f32[8,8,128]{2,1,0:T(8,128)}, u32[]{:S(2)}) copy-start(f32[8,8,128]{2,1,0:T(8,128)} %src_ref.1) | copy-start | bytes 98308
  3.4 0.8 %copy-start.4 = (f32[8,8,128]{2,1,0:T(8,128)S(1)}, f32[8,8,128]{2,1,0:T(8,128)}, u32[]{:S(2)}) copy-start(f32[8,8,128]{2,1,0:T(8,128)} %r_ref.1) | copy-start | bytes 98308

commit v2 on v1

--- a/solution.py
+++ b/solution.py
@@ -10,6 +10,7 @@
 F32 = jnp.float32
 RELAX = 0.7
 KEEP = 1.0 - RELAX
+COPIES = 208
 
 ZX = [(k, a) for k in range(4) for a in (0, 1, -1) if (k, a) != (0, 0)]
 
@@ -73,26 +74,37 @@
 
 
 def kernel(
-    src_ref, r_ref, k_ref, v_ref, f_ref, out_ref,
+    src_hbm, r_hbm, k_hbm, v_hbm, f_hbm, out_ref,
+    src_ref, r_ref, k_ref, v_ref, f_ref, in_sems,
     e0a, e0z, e0y, xb0, zlo, zhi, ylo, yhi,
     ea, ex, ey, exy, pk, pkr,
     cu, d0, va, vx, vy,
     wa, wx, wpk, wpkr,
-    ys, ylr, yhr, c1, c2, c3,
-    b1c, b1r, b1l, b1h, b1, v1p, v1q,
+    p1, s1, s1l, s1h, a2, a3, c1, c2, c3,
+    b1c, b1, v1p, v1q,
     b2c, b2r, b2l, b2h, b2, v2p, v2q,
-    b3, go_a, go_b, ssem, rsem,
+    b3, go_a, go_b, go_c, ssem, rsem,
 ):
     net = Net(ssem, rsem)
     send = net.send
     gz, gx, gy = lax.axis_index("gz"), lax.axis_index("gx"), lax.axis_index("gy")
     sx, ly = iota((8, 128), 0), iota((8, 128), 1)
 
+    fetches = [
+        pltpu.make_async_copy(here, there, in_sems.at[i])
+        for i, (here, there) in enumerate(
+            ((k_hbm, k_ref), (v_hbm, v_ref), (f_hbm, f_ref), (src_hbm, src_ref), (r_hbm, r_ref))
+        )
+    ]
+    for fetch in fetches:
+        fetch.start()
     barrier = pltpu.get_barrier_semaphore()
     greeted = [(1, 0, 0), (2, 0, 0), (3, 0, 0), (0, 1, 0), (0, -1, 0), (0, 0, 1), (0, 0, -1)]
     for offset in greeted:
         pl.semaphore_signal(barrier, inc=1, device_id=at(offset), device_id_type=MESH)
 
+    for fetch in fetches[:3]:
+        fetch.wait()
     e0a[0] = k_ref[1]
     e0a[1] = v_ref[1]
     e0a[2] = f_ref[1].astype(F32)
@@ -133,6 +145,10 @@
     wait(e0)
     for a in (2, -2):
         pl.semaphore_signal(go_a, inc=1, device_id=at((0, a, 0)), device_id_type=MESH)
+    for t in (1, -1):
+        pl.semaphore_signal(go_c, inc=1, device_id=at((0, 0, t)), device_id_type=MESH)
+    for fetch in fetches[3:]:
+        fetch.wait()
 
     both0 = jnp.where((ly & 1) == 0, ylo[...], yhi[...])
     pack = jnp.zeros((8, 128), F32)
@@ -264,53 +280,75 @@
     def rows23(pz, px):
         return mat(8, 8, lambda i, j: (i == 0) & (j < 4) & low_lanes(j, pz) & low_lanes(j >> 1, px))
 
+    def halves(block):
+        return jnp.where(own8, block[0:8], roll(block[8:16], 64, 1))
+
+    def zslot(k):
+        return (4 - k) % 4
+
+    def xplace(own, per, a):
+        return own - per * a
+
+    own8 = (ly >= 32) & (ly < 96)
     level1 = []
     for q in range(7):
         planes = [pairs(q, (cu[q, 2 * z] if q < 6 else r_ref[2 * z]), (cu[q, 2 * z + 1] if q < 6 else r_ref[2 * z + 1])) for z in range(4)]
         stacked = jnp.concatenate(planes, axis=0)
         level1.append(dot(dot(rows01(PICKS[q][1]), stacked), lanes01(PICKS[q][2])))
+    scaled1 = scaled_terms(level1, own1)
+    d1_own = scaled1[6]
+    strip = jnp.zeros((8, 128), F32)
+    for q in range(7):
+        block = halves(scaled1[q])
+        for x in range(2):
+            p1[q, 1, x, 0:4, :] = block[4 * x : 4 * x + 4]
+        if q < 6:
+            for h in range(2):
+                t = 4 * (2 * q + h)
+                moved = roll(scaled1[q][8 * h : 8 * h + 8], t - 92, 1)
+                strip = jnp.where(((ly >= t) & (ly < t + 4)) | ((ly >= t + 68) & (ly < t + 72)), moved, strip)
+    for x in range(2):
+        s1[x, 0:4, :] = strip[4 * x : 4 * x + 4]
+    c1_copies = []
+    for k, a in ZX:
+        n = 6 if a else 7
+        c1_copies.append(
+            send(
+                p1.at[pl.ds(0, n), pl.ds(1, 1), :, pl.ds(0, 4)],
+                p1.at[pl.ds(0, n), pl.ds(1 - a, 1), :, pl.ds(4 * zslot(k), 4)],
+                (k, a, 0),
+            )
+        )
+    pl.semaphore_wait(go_c, 2)
+    for k, a in [(0, 0)] + ZX:
+        for t in (1, -1):
+            there = s1l if t == 1 else s1h
+            c1_copies.append(send(s1.at[:, pl.ds(0, 4)], there.at[1 - a, :, pl.ds(4 * zslot(k), 4)], (k, a, t)))
+
     level2 = [dot(dot(rows12(PICKS[q][0], PICKS[q][1]), level1[q]), lanes12(PICKS[q][2])) for q in range(7)]
     level3 = [dot(dot(rows23(PICKS[q][0], PICKS[q][1]), level2[q]), lanes23(PICKS[q][2])) for q in range(7)]
     inside2 = (ly >= 32) & (ly < 64) & (sx < 4)
     inside3 = (ly >= 16) & (ly < 32) & (sx < 1)
-    scaled1 = scaled_terms(level1, own1)
     scaled2 = scaled_terms(level2, inside2)
     scaled3 = scaled_terms(level3, inside3)
+    group = [jnp.zeros((8, 128), F32), jnp.zeros((8, 128), F32)]
+    line = jnp.zeros((8, 128), F32)
     for q in range(7):
-        ys[pl.ds(16 * q, 16), :] = roll(scaled1[q], 64, 1)
-        ys[pl.ds(112 + 8 * q, 8), :] = roll(scaled2[q], 32, 1) + roll(scaled2[q], -32, 1)
-        ys[pl.ds(168 + 8 * q, 8), :] = roll(scaled3[q], 16, 1) + roll(scaled3[q], -16, 1)
-    stage_y = [send(ys, ylr, (0, 0, 1)), send(ys, yhr, (0, 0, -1))]
-
-    wait(stage_y)
-    lane16 = iota((16, 128), 1)
-    for q in range(7):
-        part = pl.ds(16 * q, 16)
-        merged = jnp.where(lane16 < 32, ylr[part, :], jnp.where(lane16 >= 96, yhr[part, :], scaled1[q]))
-        for x in range(4):
-            c1[q, 4 + x, 0:4, :] = merged[4 * x : 4 * x + 4]
-        part = pl.ds(112 + 8 * q, 8)
-        merged = jnp.where(ly < 32, ylr[part, :], jnp.where(ly >= 64, yhr[part, :], scaled2[q]))
+        g, j = q // 4, q % 4
+        group[g] = group[g] + roll(scaled2[q], 32 * j - 32, 1)
+        line = line + roll(scaled3[q], 16 * q - 16, 1)
+    for g in range(2):
         for x in range(2):
-            c2[q, 6 + x, 0:2, :] = merged[2 * x : 2 * x + 2]
-        part = pl.ds(168 + 8 * q, 8)
-        merged = jnp.where(ly < 16, ylr[part, :], jnp.where(ly >= 32, yhr[part, :], scaled3[q]))
-        c3[q, 0, 0:1, :] = merged[0:1]
-
-    def zslot(k):
-        return (4 - k) % 4
-
-    def xplace(own, per, a):
-        return own - per * a
-
-    c1_copies = [
-        send(c1.at[:, pl.ds(4, 4), pl.ds(0, 4)], c1.at[:, pl.ds(xplace(4, 4, a), 4), pl.ds(4 * zslot(k), 4)], (k, a, 0))
-        for k, a in ZX
-    ]
+            a2[1, 2 * g + x, 0:2, :] = group[g][2 * x : 2 * x + 2]
+    a3[1, 0:1, :] = line[0:1]
     z_copies = []
-    for k in (1, 2, 3):
-        z_copies.append(send(c2.at[:, pl.ds(6, 2), pl.ds(0, 2)], c2.at[:, pl.ds(6, 2), pl.ds(2 * zslot(k), 2)], (k, 0, 0)))
-        z_copies.append(send(c3.at[:, pl.ds(0, 1), pl.ds(0, 1)], c3.at[:, pl.ds(0, 1), pl.ds(zslot(k), 1)], (k, 0, 0)))
+    for k in range(4):
+        for t in (0, 1, -1):
+            if k or t:
+                z_copies.append(
+                    send(a2.at[pl.ds(1, 1), :, pl.ds(0, 2)], a2.at[pl.ds(1 - t, 1), :, pl.ds(2 * zslot(k), 2)], (k, 0, t))
+                )
+                z_copies.append(send(a3.at[pl.ds(1, 1), pl.ds(0, 1)], a3.at[pl.ds(1 - t, 1), pl.ds(zslot(k), 1)], (k, 0, t)))
 
     wait(r1)
     pl.semaphore_wait(go_a, 2)
@@ -374,21 +412,17 @@
         two = [(sweep_a(va, vx, vy, 2 + p, 2) - va[2 + p]) * d0[p] for p in (2 * z, 2 * z + 1)]
         planes.append(two[0] + two[1])
     rhs1 = dot(dot(rows01(None), jnp.concatenate(planes, axis=0)), lanes01(None))
-    d1_own = jnp.concatenate([c1[6, 4 + x, 0:4, :] for x in range(4)], axis=0)
-    rhs1 = jnp.where(own1, rhs1 / jnp.where(own1, d1_own, 1.0), 0.0)
-    turned = roll(rhs1, 64, 1)
-    for x in range(4):
-        b1c[4 + x, 0:4, :] = rhs1[4 * x : 4 * x + 4]
-        b1r[x, 0:4, :] = turned[4 * x : 4 * x + 4]
+    rhs1 = halves(jnp.where(own1, rhs1 / jnp.where(own1, d1_own, 1.0), 0.0))
+    for x in range(2):
+        b1c[1, 1, x, 0:4, :] = rhs1[4 * x : 4 * x + 4]
 
     r2 = []
-    for k, a in ZX:
-        there = (pl.ds(xplace(4, 4, a), 4), pl.ds(4 * zslot(k), 4))
-        r2.append(send(b1c.at[pl.ds(4, 4), pl.ds(0, 4)], b1c.at[there], (k, a, 0)))
-    for k, a in [(0, 0)] + ZX:
-        there = (pl.ds(xplace(4, 4, a), 4), pl.ds(4 * zslot(k), 4))
-        r2.append(send(b1r.at[:, pl.ds(0, 4)], b1l.at[there], (k, a, 1)))
-        r2.append(send(b1r.at[:, pl.ds(0, 4)], b1h.at[there], (k, a, -1)))
+    for t in (0, 1, -1):
+        for k, a in [(0, 0)] + ZX:
+            if (k, a, t) != (0, 0, 0):
+                r2.append(
+                    send(b1c.at[1, 1, :, pl.ds(0, 4)], b1c.at[1 - t, 1 - a, :, pl.ds(4 * zslot(k), 4)], (k, a, t))
+                )
 
     pack = jnp.zeros((8, 128), F32)
     for z in range(8):
@@ -399,9 +433,21 @@
     up0 = rim(wa, wx, wpk, wpkr)
 
     wait(z_copies)
+    for q in range(7):
+        g, j = q // 4, q % 4
+        for x in range(2):
+            low, mid, high = [roll(a2[t, 2 * g + x], 32 * t - 32 * j, 1) for t in range(3)]
+            c2[q, 6 + x] = jnp.where(ly < 32, low, jnp.where(ly < 64, mid, jnp.where(ly < 96, high, 0.0)))
     c2_copies = [
-        send(c2.at[:, pl.ds(6, 2)], c2.at[:, pl.ds(xplace(6, 2, a), 2)], (0, a, 0)) for a in (1, -1, 2, -2, 3, -3)
+        send(c2.at[pl.ds(0, 6), pl.ds(6, 2)], c2.at[pl.ds(0, 6), pl.ds(xplace(6, 2, a), 2)], (0, a, 0))
+        for a in (1, -1, 2, -2, 3, -3)
     ]
+    fields3 = []
+    for q in range(7):
+        low, mid, high = [roll(a3[t], 16 * t - 16 * q, 1) for t in range(3)]
+        fields3.append(jnp.where(ly < 16, low, jnp.where(ly < 32, mid, jnp.where(ly < 48, high, 0.0))))
+    for q in range(3):
+        c3[q, 0] = jnp.where(ly < 64, fields3[2 * q], roll(fields3[2 * q + 1], 64, 1))
 
     def sweep_l(v, b, c, x):
         here = v[x]
@@ -411,9 +457,25 @@
         )
 
     wait(c1_copies)
+    lane16 = iota((16, 128), 1)
+    own16 = (lane16 >= 32) & (lane16 < 96)
+    for i in range(3):
+        for x in range(2):
+            rims = jnp.where(lane16 < 64, s1l[i, x], s1h[i, x])
+            for q in range(6):
+                block = p1[q, i, x]
+                c1[q, 4 * i + x] = jnp.where(own16, block, roll(rims, 28 - 8 * q, 1))
+                c1[q, 4 * i + 2 + x] = jnp.where(own16, roll(block, 64, 1), roll(rims, 24 - 8 * q, 1))
+    for x in range(2):
+        block = p1[6, 1, x]
+        c1[6, 4 + x] = block
+        c1[6, 6 + x] = roll(block, 64, 1)
     wait(r2)
-    for x in range(12):
-        b1[x] = jnp.where(lane16 < 32, b1l[x], jnp.where(lane16 >= 96, b1h[x], b1c[x]))
+    for i in range(3):
+        for x in range(2):
+            low, mid, high = [b1c[t, i, x] for t in range(3)]
+            b1[4 * i + x] = jnp.where(own16, mid, roll(jnp.where(lane16 >= 64, low, high), 64, 1))
+            b1[4 * i + 2 + x] = jnp.where(own16, roll(mid, 64, 1), jnp.where(lane16 < 64, low, high))
     for x in range(1, 11):
         v1p[x] = sweep_l(b1, b1, c1, x)
     rows = []
@@ -438,7 +500,7 @@
         r3.append(send(b2r, b2h.at[there], (0, a, -1)))
     pl.semaphore_wait(go_b, 2)
     c3_copies = [
-        send(c3.at[pl.ds(0, 6), pl.ds(0, 1), pl.ds(0, 4)], c3.at[pl.ds(0, 6), pl.ds(16 - a, 1), pl.ds(0, 4)], (0, a, 0))
+        send(c3.at[:, pl.ds(0, 1), pl.ds(0, 4)], c3.at[:, pl.ds(16 - a, 1), pl.ds(0, 4)], (0, a, 0))
         for a in range(1, 16)
     ]
 
@@ -456,12 +518,15 @@
         return jnp.where(sx < 4, block, roll(block, 4, 0))
 
     inside = ly < 48
-    rhs3 = jnp.where(inside, rhs3 / jnp.where(inside, twice(c3[6, 0]), 1.0), 0.0)
+    rhs3 = jnp.where(inside, rhs3 / jnp.where(inside, twice(fields3[6]), 1.0), 0.0)
     b3[0] = rhs3
 
     r4 = [send(b3.at[pl.ds(0, 1)], b3.at[pl.ds(16 - a, 1)], (0, a, 0)) for a in range(1, 16)]
     wait(c3_copies)
-    terms3 = [[twice(c3[q, x]) for x in range(16)] for q in range(6)]
+    terms3 = []
+    for q in range(3):
+        terms3.append([twice(c3[q, x]) for x in range(16)])
+        terms3.append([roll(block, 64, 1) for block in terms3[-1]])
     wait(r4)
     rhs3 = [b3[x] for x in range(16)]
     here = rhs3
@@ -539,21 +604,24 @@
 
     tile = (8, 128)
     scratch = [
+        vmem(8, *tile), vmem(8, *tile), vmem(3, 8, *tile), vmem(3, 8, *tile), pltpu.VMEM((3, 8, *tile), jnp.int32),
+        pltpu.SemaphoreType.DMA((5,)),
         vmem(3, 8, *tile), vmem(5, *tile), vmem(*tile), vmem(3, 8, *tile), vmem(3, *tile), vmem(2, *tile), vmem(*tile), vmem(*tile),
         vmem(7, 12, *tile), vmem(7, 10, *tile), vmem(7, 10, *tile), vmem(8, *tile), vmem(*tile), vmem(10, *tile),
         vmem(6, 8, *tile), vmem(8, *tile), vmem(12, *tile), vmem(8, *tile), vmem(8, *tile),
         vmem(12, *tile), vmem(10, *tile), vmem(*tile), vmem(10, *tile),
-        vmem(224, 128), vmem(224, 128), vmem(224, 128), vmem(7, 12, 16, 128), vmem(7, 14, *tile), vmem(7, 16, *tile),
-        vmem(12, 16, 128), vmem(4, *tile), vmem(12, 16, 128), vmem(12, 16, 128), vmem(12, 16, 128), vmem(12, 16, 128), vmem(12, 16, 128),
+        vmem(7, 3, 2, 16, 128), vmem(2, *tile), vmem(3, 2, 16, 128), vmem(3, 2, 16, 128), vmem(3, 4, *tile), vmem(3, *tile),
+        vmem(7, 12, 16, 128), vmem(7, 14, *tile), vmem(3, 16, *tile),
+        vmem(3, 3, 2, 16, 128), vmem(12, 16, 128), vmem(12, 16, 128), vmem(12, 16, 128),
         vmem(14, *tile), vmem(2, *tile), vmem(14, *tile), vmem(14, *tile), vmem(14, *tile), vmem(14, *tile), vmem(14, *tile),
         vmem(16, *tile),
-        pltpu.SemaphoreType.REGULAR, pltpu.SemaphoreType.REGULAR,
-        pltpu.SemaphoreType.DMA((160,)), pltpu.SemaphoreType.DMA((160,)),
+        pltpu.SemaphoreType.REGULAR, pltpu.SemaphoreType.REGULAR, pltpu.SemaphoreType.REGULAR,
+        pltpu.SemaphoreType.DMA((COPIES,)), pltpu.SemaphoreType.DMA((COPIES,)),
     ]
     return pl.pallas_call(
         kernel,
         out_shape=jax.ShapeDtypeStruct((8, 8, 128), F32),
-        in_specs=[pl.BlockSpec(memory_space=pltpu.VMEM)] * 5,
+        in_specs=[pl.BlockSpec(memory_space=pltpu.HBM)] * 5,
         out_specs=pl.BlockSpec(memory_space=pltpu.VMEM),
         scratch_shapes=scratch,
         compiler_params=pltpu.CompilerParams(

time: 62.3 us -> 51.3 us (0.82)
  Pallas kernels: 57.1 us -> 46.1 us
    pallas_call x1, Pallas kernels: 57.1 us -> 46.1 us  [on_device(): pl.pallas_call(kernel, out_shape=jax.ShapeDtypeStruct((8, 8, 128), F32),...]
where the time goes in v2:
time: 51.3 us; the launch traced here: 51 us
  Pallas kernels  46.1 us (90%)
  local copies, waits for them, and re-layouts  4.81 us (9%)
    pallas_call x1, Pallas kernels, on_device(): pl.pallas_call(kernel, out_shape=jax.ShapeDtypeStruct((8, 8, 128), F32),...  46.1 us
    unnamed x11, local copies, waits for them, and re-layouts  4.81 us

profile of v2, /device:TPU:1, one launch (start us, length us, event | category | flops | bytes accessed | tf_op | source)
XLA Modules:
  0.0 51.0 jit_solution(9676355843244158492)
XLA Ops:
  0.0 0.0 copy-start
  0.0 0.9 %copy-done = f32[3,8,8,128]{3,2,1,0:T(8,128)S(1)} copy-done((f32[3,8,8,128]{3,2,1,0:T(8,128)S(1)}, f32[3,8,8,128]{3,2,1,0:T(8,128)}, u32[]{:S(2)}) %copy-start) | copy-done | bytes 98328
  0.9 0.0 copy-start.1
  0.9 0.9 %copy-done.1 = f32[3,8,8,128]{3,2,1,0:T(8,128)S(1)} copy-done((f32[3,8,8,128]{3,2,1,0:T(8,128)S(1)}, f32[3,8,8,128]{3,2,1,0:T(8,128)}, u32[]{:S(2)}) %copy-start.1) | copy-done | bytes 98328
  1.8 0.0 copy-start.2
  1.8 0.9 %copy-done.2 = s32[3,8,8,128]{3,2,1,0:T(8,128)S(1)} copy-done((s32[3,8,8,128]{3,2,1,0:T(8,128)S(1)}, s32[3,8,8,128]{3,2,1,0:T(8,128)}, u32[]{:S(2)}) %copy-start.2) | copy-done | bytes 98328
  2.7 0.0 copy-start.3
  2.7 0.8 %copy-done.3 = f32[8,8,128]{2,1,0:T(8,128)S(1)} copy-done((f32[8,8,128]{2,1,0:T(8,128)S(1)}, f32[8,8,128]{2,1,0:T(8,128)}, u32[]{:S(2)}) %copy-start.3) | copy-done | bytes 32792
  3.4 0.0 copy-start.4
  3.4 0.8 %copy-done.4 = f32[8,8,128]{2,1,0:T(8,128)S(1)} copy-done((f32[8,8,128]{2,1,0:T(8,128)S(1)}, f32[8,8,128]{2,1,0:T(8,128)}, u32[]{:S(2)}) %copy-start.4) | copy-done | bytes 32792
  4.2 46.1 %shard_map.55 = f32[8,8,128]{2,1,0:T(8,128)S(1)} custom-call(f32[8,8,128]{2,1,0:T(8,128)S(1)} %copy-done.3, f32[8,8,128]{2,1,0:T(8,128)S(1)} %copy-done.4, f32[3,8,8,128]{3,2,1,0:T(8,128)S(1)} %copy-done, f32[3,8,8,128]{3,2,1,0:T(8,128)S(1)} %copy-done.1, s32[3,8,8,128]{3,2,1,0:T(8,128)S(1)} %copy-done.2), custom_call_target="tpu_custom_call" | custom-call | tf_op jit(solution)/shard_map/pallas_call | solution.py:621
  50.4 0.6 %copy.7 = f32[8,8,128]{2,1,0:T(8,128)} copy(f32[8,8,128]{2,1,0:T(8,128)S(1)} %shard_map.55) | data formatting | bytes 65536
Async XLA Ops:
  0.0 0.9 %copy-start = (f32[3,8,8,128]{3,2,1,0:T(8,128)S(1)}, f32[3,8,8,128]{3,2,1,0:T(8,128)}, u32[]{:S(2)}) copy-start(f32[3,8,8,128]{3,2,1,0:T(8,128)} %k_hbm.1) | copy-start | bytes 294916
  0.9 0.9 %copy-start.1 = (f32[3,8,8,128]{3,2,1,0:T(8,128)S(1)}, f32[3,8,8,128]{3,2,1,0:T(8,128)}, u32[]{:S(2)}) copy-start(f32[3,8,8,128]{3,2,1,0:T(8,128)} %v_hbm.1) | copy-start | bytes 294916
  1.8 0.9 %copy-start.2 = (s32[3,8,8,128]{3,2,1,0:T(8,128)S(1)}, s32[3,8,8,128]{3,2,1,0:T(8,128)}, u32[]{:S(2)}) copy-start(s32[3,8,8,128]{3,2,1,0:T(8,128)} %f_hbm.1) | copy-start | bytes 294916
  2.7 0.8 %copy-start.3 = (f32[8,8,128]{2,1,0:T(8,128)S(1)}, f32[8,8,128]{2,1,0:T(8,128)}, u32[]{:S(2)}) copy-start(f32[8,8,128]{2,1,0:T(8,128)} %src_hbm.1) | copy-start | bytes 98308
  3.4 0.8 %copy-start.4 = (f32[8,8,128]{2,1,0:T(8,128)S(1)}, f32[8,8,128]{2,1,0:T(8,128)}, u32[]{:S(2)}) copy-start(f32[8,8,128]{2,1,0:T(8,128)} %r_hbm.1) | copy-start | bytes 98308

commit v3 on v2

--- a/solution.py
+++ b/solution.py
@@ -10,40 +10,61 @@
 F32 = jnp.float32
 RELAX = 0.7
 KEEP = 1.0 - RELAX
-COPIES = 208
+GROUPS = 10
 
 ZX = [(k, a) for k in range(4) for a in (0, 1, -1) if (k, a) != (0, 0)]
 
 
-def at(offset):
-    return {
-        name: lax.rem(lax.axis_index(name) + (step + size), size)
-        for (name, size), step in zip(SIZES, offset)
-    }
-
-
 class Net:
-    def __init__(self, send_sems, recv_sems):
-        self.send_sems, self.recv_sems, self.copies = send_sems, recv_sems, []
-
-    def send(self, src, dst, offset):
-        index = len(self.copies)
-        copy = pltpu.make_async_remote_copy(
+    def __init__(self, tally, send_sems, recv_sems):
+        self.tally, self.send_sems, self.recv_sems = tally, send_sems, recv_sems
+        self.rows, self.places = [], {}
+        for name, size in SIZES:
+            here = lax.axis_index(name)
+            for step in range(size):
+                self.places[name, step] = (here + step) & (size - 1) if step else here
+
+    def at(self, offset):
+        return {name: self.places[name, step % size] for (name, size), step in zip(SIZES, offset)}
+
+    def signal(self, sem, offset):
+        pl.semaphore_signal(sem, inc=1, device_id=self.at(offset), device_id_type=MESH)
+
+    def group(self):
+        self.rows.append(0)
+        return len(self.rows) - 1
+
+    def send(self, group, src, dst, offset):
+        size = 1
+        for n in src.shape:
+            size *= n
+        self.rows[group] += size // 128
+        pltpu.make_async_remote_copy(
             src_ref=src,
             dst_ref=dst,
-            send_sem=self.send_sems.at[index],
-            recv_sem=self.recv_sems.at[index],
-            device_id=at(offset),
+            send_sem=self.send_sems.at[group],
+            recv_sem=self.recv_sems.at[group],
+            device_id=self.at(offset),
+            device_id_type=MESH,
+        ).start()
+
+    def whole(self, group):
+        part = self.tally.at[pl.ds(0, self.rows[group])]
+        return pltpu.make_async_remote_copy(
+            src_ref=part,
+            dst_ref=part,
+            send_sem=self.send_sems.at[group],
+            recv_sem=self.recv_sems.at[group],
+            device_id=self.at((0, 0, 1)),
             device_id_type=MESH,
         )
-        copy.start()
-        self.copies.append(copy)
-        return copy
-
-
-def wait(copies):
-    for copy in copies:
-        copy.wait_recv()
+
+    def wait(self, group):
+        self.whole(group).wait_recv()
+
+    def finish(self):
+        for group in range(len(self.rows)):
+            self.whole(group).wait_send()
 
 
 def iota(shape, dim):
@@ -54,8 +75,28 @@
     return jnp.where(where(iota((rows, cols), 0), iota((rows, cols), 1)), 1.0, 0.0).astype(F32)
 
 
-def dot(a, b):
-    return jnp.dot(a, b, preferred_element_type=F32, precision=lax.Precision.HIGHEST)
+def split(x):
+    high = x.astype(jnp.bfloat16)
+    return high, (x - high.astype(F32)).astype(jnp.bfloat16)
+
+
+def dot(a, b, ones):
+    if ones:
+        b = b.astype(jnp.bfloat16)
+        pairs = [(part, b) for part in split(a)]
+    else:
+        a = a.astype(jnp.bfloat16)
+        pairs = [(a, part) for part in split(b)]
+    high, low = [jnp.dot(x, y, preferred_element_type=F32) for x, y in pairs]
+    return high + low
+
+
+def left(a, b):
+    return dot(a, b, 0)
+
+
+def right(a, b):
+    return dot(a, b, 1)
 
 
 def roll(x, shift, axis):
@@ -83,10 +124,10 @@
     p1, s1, s1l, s1h, a2, a3, c1, c2, c3,
     b1c, b1, v1p, v1q,
     b2c, b2r, b2l, b2h, b2, v2p, v2q,
-    b3, go_a, go_b, go_c, ssem, rsem,
+    b3, go_a, go_b, go_c, tally, ssem, rsem,
 ):
-    net = Net(ssem, rsem)
-    send = net.send
+    net = Net(tally, ssem, rsem)
+    send, wait = net.send, net.wait
     gz, gx, gy = lax.axis_index("gz"), lax.axis_index("gx"), lax.axis_index("gy")
     sx, ly = iota((8, 128), 0), iota((8, 128), 1)
 
@@ -101,7 +142,7 @@
     barrier = pltpu.get_barrier_semaphore()
     greeted = [(1, 0, 0), (2, 0, 0), (3, 0, 0), (0, 1, 0), (0, -1, 0), (0, 0, 1), (0, 0, -1)]
     for offset in greeted:
-        pl.semaphore_signal(barrier, inc=1, device_id=at(offset), device_id_type=MESH)
+        net.signal(barrier, offset)
 
     for fetch in fetches[:3]:
         fetch.wait()
@@ -121,14 +162,13 @@
             packed = jnp.where((ly >= start) & (ly < start + 2), moved, packed)
     e0y[...] = packed
     pl.semaphore_wait(barrier, len(greeted))
-    e0 = [
-        send(e0a.at[:, :, pl.ds(7, 1), :], xb0.at[:, :, pl.ds(7, 1), :], (0, 1, 0)),
-        send(e0a.at[pl.ds(0, 2), :, pl.ds(0, 1), :], xb0.at[pl.ds(0, 2), :, pl.ds(0, 1), :], (0, -1, 0)),
-        send(e0z.at[pl.ds(0, 3)], zlo, (1, 0, 0)),
-        send(e0z.at[pl.ds(3, 2)], zhi, (-1, 0, 0)),
-        send(e0y, ylo, (0, 0, 1)),
-        send(e0y, yhi, (0, 0, -1)),
-    ]
+    e0 = net.group()
+    send(e0, e0a.at[:, :, pl.ds(7, 1), :], xb0.at[:, :, pl.ds(7, 1), :], (0, 1, 0))
+    send(e0, e0a.at[pl.ds(0, 2), :, pl.ds(0, 1), :], xb0.at[pl.ds(0, 2), :, pl.ds(0, 1), :], (0, -1, 0))
+    send(e0, e0z.at[pl.ds(0, 3)], zlo, (1, 0, 0))
+    send(e0, e0z.at[pl.ds(3, 2)], zhi, (-1, 0, 0))
+    send(e0, e0y, ylo, (0, 0, 1))
+    send(e0, e0y, yhi, (0, 0, -1))
 
     def xprev(a, b):
         return roll(jnp.where(sx == 7, b, a), 1, 0)
@@ -144,9 +184,9 @@
 
     wait(e0)
     for a in (2, -2):
-        pl.semaphore_signal(go_a, inc=1, device_id=at((0, a, 0)), device_id_type=MESH)
+        net.signal(go_a, (0, a, 0))
     for t in (1, -1):
-        pl.semaphore_signal(go_c, inc=1, device_id=at((0, 0, t)), device_id_type=MESH)
+        net.signal(go_c, (0, 0, t))
     for fetch in fetches[3:]:
         fetch.wait()
 
@@ -219,31 +259,27 @@
 
     diagonal_y = [(0, 0, 1), (0, 0, -1)] + [(s, 0, t) for s in (1, -1) for t in (1, -1)] + [(0, s, t) for s in (1, -1) for t in (1, -1)]
 
-    def rim(a, x, p, pr):
-        copies = []
+    def rim(group, a, x, p, pr):
         for s in (1, -1):
             mine, theirs = (8, 0) if s == 1 else (2, 10)
-            copies.append(send(a.at[pl.ds(mine, 2)], a.at[pl.ds(theirs, 2)], (s, 0, 0)))
+            send(group, a.at[pl.ds(mine, 2)], a.at[pl.ds(theirs, 2)], (s, 0, 0))
             row = 6 if s == 1 else 0
-            copies.append(send(a.at[pl.ds(2, 8), pl.ds(row, 2)], x.at[pl.ds(1, 8), pl.ds(row, 2)], (0, s, 0)))
+            send(group, a.at[pl.ds(2, 8), pl.ds(row, 2)], x.at[pl.ds(1, 8), pl.ds(row, 2)], (0, s, 0))
         for i, offset in enumerate(diagonal_y):
-            copies.append(send(p, pr.at[i], offset))
+            send(group, p, pr.at[i], offset)
         for s in (1, -1):
             for t in (1, -1):
                 plane, row = (9 if s == 1 else 2), (7 if t == 1 else 0)
-                copies.append(
-                    send(a.at[pl.ds(plane, 1), pl.ds(row, 1)], x.at[pl.ds(0 if s == 1 else 9, 1), pl.ds(row, 1)], (s, t, 0))
-                )
-        return copies
-
-    r1 = []
+                there = x.at[pl.ds(0 if s == 1 else 9, 1), pl.ds(row, 1)]
+                send(group, a.at[pl.ds(plane, 1), pl.ds(row, 1)], there, (s, t, 0))
+
+    r1 = net.group()
     for s in (1, -1):
         mine, theirs, row = (9, 1, 7) if s == 1 else (2, 10, 0)
-        r1.append(send(ea.at[pl.ds(1, 6), pl.ds(mine, 1)], ea.at[pl.ds(1, 6), pl.ds(theirs, 1)], (s, 0, 0)))
-        r1.append(
-            send(ea.at[pl.ds(1, 6), pl.ds(2, 8), pl.ds(row, 1)], ex.at[pl.ds(1, 6), pl.ds(1, 8), pl.ds(row, 1)], (0, s, 0))
-        )
-    r1 += rim(ea.at[0], ex.at[0], pk, pkr)
+        send(r1, ea.at[pl.ds(1, 6), pl.ds(mine, 1)], ea.at[pl.ds(1, 6), pl.ds(theirs, 1)], (s, 0, 0))
+        there = ex.at[pl.ds(1, 6), pl.ds(1, 8), pl.ds(row, 1)]
+        send(r1, ea.at[pl.ds(1, 6), pl.ds(2, 8), pl.ds(row, 1)], there, (0, s, 0))
+    rim(r1, ea.at[0], ex.at[0], pk, pkr)
 
     own1 = (iota((16, 128), 1) >= 32) & (iota((16, 128), 1) < 96)
 
@@ -294,7 +330,7 @@
     for q in range(7):
         planes = [pairs(q, (cu[q, 2 * z] if q < 6 else r_ref[2 * z]), (cu[q, 2 * z + 1] if q < 6 else r_ref[2 * z + 1])) for z in range(4)]
         stacked = jnp.concatenate(planes, axis=0)
-        level1.append(dot(dot(rows01(PICKS[q][1]), stacked), lanes01(PICKS[q][2])))
+        level1.append(right(left(rows01(PICKS[q][1]), stacked), lanes01(PICKS[q][2])))
     scaled1 = scaled_terms(level1, own1)
     d1_own = scaled1[6]
     strip = jnp.zeros((8, 128), F32)
@@ -309,24 +345,19 @@
                 strip = jnp.where(((ly >= t) & (ly < t + 4)) | ((ly >= t + 68) & (ly < t + 72)), moved, strip)
     for x in range(2):
         s1[x, 0:4, :] = strip[4 * x : 4 * x + 4]
-    c1_copies = []
+    c1_copies = net.group()
     for k, a in ZX:
         n = 6 if a else 7
-        c1_copies.append(
-            send(
-                p1.at[pl.ds(0, n), pl.ds(1, 1), :, pl.ds(0, 4)],
-                p1.at[pl.ds(0, n), pl.ds(1 - a, 1), :, pl.ds(4 * zslot(k), 4)],
-                (k, a, 0),
-            )
-        )
+        there = p1.at[pl.ds(0, n), pl.ds(1 - a, 1), :, pl.ds(4 * zslot(k), 4)]
+        send(c1_copies, p1.at[pl.ds(0, n), pl.ds(1, 1), :, pl.ds(0, 4)], there, (k, a, 0))
     pl.semaphore_wait(go_c, 2)
     for k, a in [(0, 0)] + ZX:
         for t in (1, -1):
             there = s1l if t == 1 else s1h
-            c1_copies.append(send(s1.at[:, pl.ds(0, 4)], there.at[1 - a, :, pl.ds(4 * zslot(k), 4)], (k, a, t)))
-
-    level2 = [dot(dot(rows12(PICKS[q][0], PICKS[q][1]), level1[q]), lanes12(PICKS[q][2])) for q in range(7)]
-    level3 = [dot(dot(rows23(PICKS[q][0], PICKS[q][1]), level2[q]), lanes23(PICKS[q][2])) for q in range(7)]
+            send(c1_copies, s1.at[:, pl.ds(0, 4)], there.at[1 - a, :, pl.ds(4 * zslot(k), 4)], (k, a, t))
+
+    level2 = [right(left(rows12(PICKS[q][0], PICKS[q][1]), level1[q]), lanes12(PICKS[q][2])) for q in range(7)]
+    level3 = [right(left(rows23(PICKS[q][0], PICKS[q][1]), level2[q]), lanes23(PICKS[q][2])) for q in range(7)]
     inside2 = (ly >= 32) & (ly < 64) & (sx < 4)
     inside3 = (ly >= 16) & (ly < 32) & (sx < 1)
     scaled2 = scaled_terms(level2, inside2)
@@ -341,19 +372,18 @@
         for x in range(2):
             a2[1, 2 * g + x, 0:2, :] = group[g][2 * x : 2 * x + 2]
     a3[1, 0:1, :] = line[0:1]
-    z_copies = []
+    z_copies = net.group()
     for k in range(4):
         for t in (0, 1, -1):
             if k or t:
-                z_copies.append(
-                    send(a2.at[pl.ds(1, 1), :, pl.ds(0, 2)], a2.at[pl.ds(1 - t, 1), :, pl.ds(2 * zslot(k), 2)], (k, 0, t))
-                )
-                z_copies.append(send(a3.at[pl.ds(1, 1), pl.ds(0, 1)], a3.at[pl.ds(1 - t, 1), pl.ds(zslot(k), 1)], (k, 0, t)))
+                there = a2.at[pl.ds(1 - t, 1), :, pl.ds(2 * zslot(k), 2)]
+                send(z_copies, a2.at[pl.ds(1, 1), :, pl.ds(0, 2)], there, (k, 0, t))
+                send(z_copies, a3.at[pl.ds(1, 1), pl.ds(0, 1)], a3.at[pl.ds(1 - t, 1), pl.ds(zslot(k), 1)], (k, 0, t))
 
     wait(r1)
     pl.semaphore_wait(go_a, 2)
     for a in (4, -4):
-        pl.semaphore_signal(go_b, inc=1, device_id=at((0, a, 0)), device_id_type=MESH)
+        net.signal(go_b, (0, a, 0))
 
     def unpack(pr, y, xy):
         from_low = (ly & jnp.where(ly < 32, 2, 1)) == 0
@@ -411,18 +441,17 @@
     for z in range(4):
         two = [(sweep_a(va, vx, vy, 2 + p, 2) - va[2 + p]) * d0[p] for p in (2 * z, 2 * z + 1)]
         planes.append(two[0] + two[1])
-    rhs1 = dot(dot(rows01(None), jnp.concatenate(planes, axis=0)), lanes01(None))
+    rhs1 = right(left(rows01(None), jnp.concatenate(planes, axis=0)), lanes01(None))
     rhs1 = halves(jnp.where(own1, rhs1 / jnp.where(own1, d1_own, 1.0), 0.0))
     for x in range(2):
         b1c[1, 1, x, 0:4, :] = rhs1[4 * x : 4 * x + 4]
 
-    r2 = []
+    r2 = net.group()
     for t in (0, 1, -1):
         for k, a in [(0, 0)] + ZX:
             if (k, a, t) != (0, 0, 0):
-                r2.append(
-                    send(b1c.at[1, 1, :, pl.ds(0, 4)], b1c.at[1 - t, 1 - a, :, pl.ds(4 * zslot(k), 4)], (k, a, t))
-                )
+                there = b1c.at[1 - t, 1 - a, :, pl.ds(4 * zslot(k), 4)]
+                send(r2, b1c.at[1, 1, :, pl.ds(0, 4)], there, (k, a, t))
 
     pack = jnp.zeros((8, 128), F32)
     for z in range(8):
@@ -430,7 +459,8 @@
         wa[2 + z] = plane
         pack = jnp.where((ly >= 4 * z) & (ly < 4 * z + 4), roll(plane, 4 * z + 2, 1), pack)
     wpk[...] = pack
-    up0 = rim(wa, wx, wpk, wpkr)
+    up0 = net.group()
+    rim(up0, wa, wx, wpk, wpkr)
 
     wait(z_copies)
     for q in range(7):
@@ -438,10 +468,9 @@
         for x in range(2):
             low, mid, high = [roll(a2[t, 2 * g + x], 32 * t - 32 * j, 1) for t in range(3)]
             c2[q, 6 + x] = jnp.where(ly < 32, low, jnp.where(ly < 64, mid, jnp.where(ly < 96, high, 0.0)))
-    c2_copies = [
-        send(c2.at[pl.ds(0, 6), pl.ds(6, 2)], c2.at[pl.ds(0, 6), pl.ds(xplace(6, 2, a), 2)], (0, a, 0))
-        for a in (1, -1, 2, -2, 3, -3)
-    ]
+    c2_copies = net.group()
+    for a in (1, -1, 2, -2, 3, -3):
+        send(c2_copies, c2.at[pl.ds(0, 6), pl.ds(6, 2)], c2.at[pl.ds(0, 6), pl.ds(xplace(6, 2, a), 2)], (0, a, 0))
     fields3 = []
     for q in range(7):
         low, mid, high = [roll(a3[t], 16 * t - 16 * q, 1) for t in range(3)]
@@ -482,27 +511,26 @@
     for x in range(2):
         two = [(sweep_l(v1p, b1, c1, p) - v1p[p]) * c1[6, p] for p in (4 + 2 * x, 5 + 2 * x)]
         rows.append(two[0] + two[1])
-    rows = dot(jnp.concatenate(rows, axis=0), lanes12(None))
+    rows = right(jnp.concatenate(rows, axis=0), lanes12(None))
     halve = mat(8, 16, lambda i, j: (j >> 1) == i)
     for x in range(2):
         inside = (ly >= 32) & (ly < 64)
-        rhs2 = dot(halve, rows[16 * x : 16 * x + 16])
+        rhs2 = left(halve, rows[16 * x : 16 * x + 16])
         rhs2 = jnp.where(inside, rhs2 / jnp.where(inside, c2[6, 6 + x], 1.0), 0.0)
         b2c[6 + x] = rhs2
         b2r[x] = roll(rhs2, 32, 1) + roll(rhs2, -32, 1)
 
-    r3 = []
+    r3 = net.group()
     for a in (0, 1, -1, 2, -2, 3, -3):
         there = pl.ds(xplace(6, 2, a), 2)
         if a:
-            r3.append(send(b2c.at[pl.ds(6, 2)], b2c.at[there], (0, a, 0)))
-        r3.append(send(b2r, b2l.at[there], (0, a, 1)))
-        r3.append(send(b2r, b2h.at[there], (0, a, -1)))
+            send(r3, b2c.at[pl.ds(6, 2)], b2c.at[there], (0, a, 0))
+        send(r3, b2r, b2l.at[there], (0, a, 1))
+        send(r3, b2r, b2h.at[there], (0, a, -1))
     pl.semaphore_wait(go_b, 2)
-    c3_copies = [
-        send(c3.at[:, pl.ds(0, 1), pl.ds(0, 4)], c3.at[:, pl.ds(16 - a, 1), pl.ds(0, 4)], (0, a, 0))
-        for a in range(1, 16)
-    ]
+    c3_copies = net.group()
+    for a in range(1, 16):
+        send(c3_copies, c3.at[:, pl.ds(0, 1), pl.ds(0, 4)], c3.at[:, pl.ds(16 - a, 1), pl.ds(0, 4)], (0, a, 0))
 
     wait(c2_copies)
     wait(r3)
@@ -511,8 +539,8 @@
     for x in range(2, 12):
         v2p[x] = sweep_l(b2, b2, c2, x)
     two = [(sweep_l(v2p, b2, c2, p) - v2p[p]) * c2[6, p] for p in (6, 7)]
-    rows = dot(two[0] + two[1], mat(128, 128, lambda i, j: (j == (i >> 1)) & (i < 96)))
-    rhs3 = dot(mat(8, 8, lambda i, j: (j >> 1) == (i & 3)), rows)
+    rows = right(two[0] + two[1], mat(128, 128, lambda i, j: (j == (i >> 1)) & (i < 96)))
+    rhs3 = left(mat(8, 8, lambda i, j: (j >> 1) == (i & 3)), rows)
 
     def twice(block):
         return jnp.where(sx < 4, block, roll(block, 4, 0))
@@ -521,7 +549,9 @@
     rhs3 = jnp.where(inside, rhs3 / jnp.where(inside, twice(fields3[6]), 1.0), 0.0)
     b3[0] = rhs3
 
-    r4 = [send(b3.at[pl.ds(0, 1)], b3.at[pl.ds(16 - a, 1)], (0, a, 0)) for a in range(1, 16)]
+    r4 = net.group()
+    for a in range(1, 16):
+        send(r4, b3.at[pl.ds(0, 1)], b3.at[pl.ds(16 - a, 1)], (0, a, 0))
     wait(c3_copies)
     terms3 = []
     for q in range(3):
@@ -539,9 +569,9 @@
             for x in range(16)
         ]
 
-    wide = dot(mat(8, 8, lambda i, j: j == (i >> 1)), jnp.concatenate([here[(X + 16) % 16] for X in range(-2, 3)], axis=1))
+    wide = left(mat(8, 8, lambda i, j: j == (i >> 1)), jnp.concatenate([here[(X + 16) % 16] for X in range(-2, 3)], axis=1))
     wide = jnp.concatenate([wide[:, 128 * i : 128 * i + 128] for i in range(5)], axis=0)
-    wide = dot(wide, mat(128, 128, lambda i, j: (i == (j >> 1)) & (j < 96)))
+    wide = right(wide, mat(128, 128, lambda i, j: (i == (j >> 1)) & (j < 96)))
     for x in range(2, 12):
         i = (x >> 1) - 1
         v2p[x] = v2p[x] + wide[8 * i : 8 * i + 8]
@@ -549,8 +579,8 @@
         v2q[x] = sweep_l(v2p, b2, c2, x)
     ups = [sweep_l(v2q, b2, c2, x) for x in range(4, 10)]
 
-    wide = dot(jnp.concatenate(ups, axis=0), mat(128, 128, lambda i, j: i == 16 + (j >> 1)))
-    wide = dot(mat(16, 8, lambda i, j: j == (i >> 1)), jnp.concatenate([wide[8 * i : 8 * i + 8] for i in range(6)], axis=1))
+    wide = right(jnp.concatenate(ups, axis=0), mat(128, 128, lambda i, j: i == 16 + (j >> 1)))
+    wide = left(mat(16, 8, lambda i, j: j == (i >> 1)), jnp.concatenate([wide[8 * i : 8 * i + 8] for i in range(6)], axis=1))
     for x in range(1, 11):
         i = x >> 1
         v1p[x] = v1p[x] + wide[:, 128 * i : 128 * i + 128]
@@ -571,8 +601,8 @@
         )
         return main | beside
 
-    wide = dot(jnp.concatenate(ups, axis=0), mat(128, 256, lanes10))
-    wide = dot(mat(176, 96, rows10), wide)
+    wide = right(jnp.concatenate(ups, axis=0), mat(128, 256, lanes10))
+    wide = left(mat(176, 96, rows10), wide)
     wait(up0)
     low = (ly & 2) == 0
     beside = jnp.where(low, wpkr[0], wpkr[1])
@@ -594,8 +624,7 @@
     rim_sweep(a, x, y, xy)
     for z in range(8):
         out_ref[z] = sweep_a(va, vx, vy, 2 + z, 2)
-    for copy in net.copies:
-        copy.wait_send()
+    net.finish()
 
 
 def on_device(source, decay_rate, dispersion, velocity, upwind):
@@ -616,7 +645,7 @@
         vmem(14, *tile), vmem(2, *tile), vmem(14, *tile), vmem(14, *tile), vmem(14, *tile), vmem(14, *tile), vmem(14, *tile),
         vmem(16, *tile),
         pltpu.SemaphoreType.REGULAR, pltpu.SemaphoreType.REGULAR, pltpu.SemaphoreType.REGULAR,
-        pltpu.SemaphoreType.DMA((COPIES,)), pltpu.SemaphoreType.DMA((COPIES,)),
+        vmem(768, 128), pltpu.SemaphoreType.DMA((GROUPS,)), pltpu.SemaphoreType.DMA((GROUPS,)),
     ]
     return pl.pallas_call(
         kernel,

time: 51.3 us -> 47.6 us (0.928)
  Pallas kernels: 46.1 us -> 42.5 us
    pallas_call x1, Pallas kernels: 46.1 us -> 42.5 us  [on_device(): pl.pallas_call(kernel, out_shape=jax.ShapeDtypeStruct((8, 8, 128), F32),...]
where the time goes in v3:
time: 47.6 us; the launch traced here: 47.3 us
  Pallas kernels  42.5 us (89%)
  local copies, waits for them, and re-layouts  4.81 us (10%)
    pallas_call x1, Pallas kernels, on_device(): pl.pallas_call(kernel, out_shape=jax.ShapeDtypeStruct((8, 8, 128), F32),...  42.5 us
    unnamed x11, local copies, waits for them, and re-layouts  4.81 us

profile of v3, /device:TPU:1, one launch (start us, length us, event | category | flops | bytes accessed | tf_op | source)
XLA Modules:
  0.0 47.3 jit_solution(2600565441430548447)
XLA Ops:
  0.0 0.0 copy-start
  0.0 0.9 %copy-done = f32[3,8,8,128]{3,2,1,0:T(8,128)S(1)} copy-done((f32[3,8,8,128]{3,2,1,0:T(8,128)S(1)}, f32[3,8,8,128]{3,2,1,0:T(8,128)}, u32[]{:S(2)}) %copy-start) | copy-done | bytes 98328
  0.9 0.0 copy-start.1
  0.9 0.9 %copy-done.1 = f32[3,8,8,128]{3,2,1,0:T(8,128)S(1)} copy-done((f32[3,8,8,128]{3,2,1,0:T(8,128)S(1)}, f32[3,8,8,128]{3,2,1,0:T(8,128)}, u32[]{:S(2)}) %copy-start.1) | copy-done | bytes 98328
  1.8 0.0 copy-start.2
  1.8 0.9 %copy-done.2 = s32[3,8,8,128]{3,2,1,0:T(8,128)S(1)} copy-done((s32[3,8,8,128]{3,2,1,0:T(8,128)S(1)}, s32[3,8,8,128]{3,2,1,0:T(8,128)}, u32[]{:S(2)}) %copy-start.2) | copy-done | bytes 98328
  2.7 0.0 copy-start.3
  2.7 0.8 %copy-done.3 = f32[8,8,128]{2,1,0:T(8,128)S(1)} copy-done((f32[8,8,128]{2,1,0:T(8,128)S(1)}, f32[8,8,128]{2,1,0:T(8,128)}, u32[]{:S(2)}) %copy-start.3) | copy-done | bytes 32792
  3.4 0.0 copy-start.4
  3.4 0.8 %copy-done.4 = f32[8,8,128]{2,1,0:T(8,128)S(1)} copy-done((f32[8,8,128]{2,1,0:T(8,128)S(1)}, f32[8,8,128]{2,1,0:T(8,128)}, u32[]{:S(2)}) %copy-start.4) | copy-done | bytes 32792
  4.2 42.5 %shard_map.55 = f32[8,8,128]{2,1,0:T(8,128)S(1)} custom-call(f32[8,8,128]{2,1,0:T(8,128)S(1)} %copy-done.3, f32[8,8,128]{2,1,0:T(8,128)S(1)} %copy-done.4, f32[3,8,8,128]{3,2,1,0:T(8,128)S(1)} %copy-done, f32[3,8,8,128]{3,2,1,0:T(8,128)S(1)} %copy-done.1, s32[3,8,8,128]{3,2,1,0:T(8,128)S(1)} %copy-done.2), custom_call_target="tpu_custom_call" | custom-call | tf_op jit(solution)/shard_map/pallas_call | solution.py:650
  46.7 0.6 %copy.7 = f32[8,8,128]{2,1,0:T(8,128)} copy(f32[8,8,128]{2,1,0:T(8,128)S(1)} %shard_map.55) | data formatting | bytes 65536
Async XLA Ops:
  0.0 0.9 %copy-start = (f32[3,8,8,128]{3,2,1,0:T(8,128)S(1)}, f32[3,8,8,128]{3,2,1,0:T(8,128)}, u32[]{:S(2)}) copy-start(f32[3,8,8,128]{3,2,1,0:T(8,128)} %k_hbm.1) | copy-start | bytes 294916
  0.9 0.9 %copy-start.1 = (f32[3,8,8,128]{3,2,1,0:T(8,128)S(1)}, f32[3,8,8,128]{3,2,1,0:T(8,128)}, u32[]{:S(2)}) copy-start(f32[3,8,8,128]{3,2,1,0:T(8,128)} %v_hbm.1) | copy-start | bytes 294916
  1.8 0.9 %copy-start.2 = (s32[3,8,8,128]{3,2,1,0:T(8,128)S(1)}, s32[3,8,8,128]{3,2,1,0:T(8,128)}, u32[]{:S(2)}) copy-start(s32[3,8,8,128]{3,2,1,0:T(8,128)} %f_hbm.1) | copy-start | bytes 294916
  2.7 0.8 %copy-start.3 = (f32[8,8,128]{2,1,0:T(8,128)S(1)}, f32[8,8,128]{2,1,0:T(8,128)}, u32[]{:S(2)}) copy-start(f32[8,8,128]{2,1,0:T(8,128)} %src_hbm.1) | copy-start | bytes 98308
  3.4 0.8 %copy-start.4 = (f32[8,8,128]{2,1,0:T(8,128)S(1)}, f32[8,8,128]{2,1,0:T(8,128)}, u32[]{:S(2)}) copy-start(f32[8,8,128]{2,1,0:T(8,128)} %r_hbm.1) | copy-start | bytes 98308

commit v4 on v3

--- a/solution.py
+++ b/solution.py
@@ -653,9 +653,7 @@
         in_specs=[pl.BlockSpec(memory_space=pltpu.HBM)] * 5,
         out_specs=pl.BlockSpec(memory_space=pltpu.VMEM),
         scratch_shapes=scratch,
-        compiler_params=pltpu.CompilerParams(
-            collective_id=0, has_side_effects=True, vmem_limit_bytes=32 * 1024 * 1024
-        ),
+        compiler_params=pltpu.CompilerParams(collective_id=0, has_side_effects=True),
     )(source, decay_rate, dispersion, velocity, upwind)
 
 

time: 47.6 us -> 44.2 us (0.929)
  local copies, waits for them, and re-layouts: 4.81 us -> 1.38 us
    unnamed x11 -> x1, local copies, waits for them, and re-layouts: 4.81 us -> 1.38 us
where the time goes in v4:
time: 44.2 us; the launch traced here: 44 us
  Pallas kernels  42.6 us (96%)
  local copies, waits for them, and re-layouts  1.38 us (3%)
    pallas_call x1, Pallas kernels, on_device(): pl.pallas_call(kernel, out_shape=jax.ShapeDtypeStruct((8, 8, 128), F32),...  42.6 us
    unnamed x1, local copies, waits for them, and re-layouts  1.38 us

profile of v4, /device:TPU:1, one launch (start us, length us, event | category | flops | bytes accessed | tf_op | source)
XLA Modules:
  0.0 44.0 jit_solution(8765103674678532675)
XLA Ops:
  0.0 42.6 %shard_map.55 = f32[8,8,128]{2,1,0:T(8,128)} custom-call(f32[8,8,128]{2,1,0:T(8,128)} %src_hbm.1, f32[8,8,128]{2,1,0:T(8,128)} %r_hbm.1, f32[3,8,8,128]{3,2,1,0:T(8,128)} %k_hbm.1, f32[3,8,8,128]{3,2,1,0:T(8,128)} %v_hbm.1, s32[3,8,8,128]{3,2,1,0:T(8,128)} %f_hbm.1), custom_call_target="tpu_custom_call" | custom-call | tf_op jit(solution)/shard_map/pallas_call | solution.py:650
  42.6 1.4 %copy.7 = f32[8,8,128]{2,1,0:T(8,128)} copy(f32[8,8,128]{2,1,0:T(8,128)} %shard_map.55) | data formatting | bytes 65536

commit v5 on v4

--- a/solution.py
+++ b/solution.py
@@ -13,6 +13,14 @@
 GROUPS = 10
 
 ZX = [(k, a) for k in range(4) for a in (0, 1, -1) if (k, a) != (0, 0)]
+
+
+def hops(offset):
+    return sum(min(step % size, -step % size) * (1 if size < 16 else 0.5) for (_, size), step in zip(SIZES, offset))
+
+
+NEAR_27 = sorted(((k, a, t) for k, a in [(0, 0)] + ZX for t in (0, 1, -1)), key=hops, reverse=True)
+ALONG_X = sorted(range(1, 16), key=lambda a: min(a, 16 - a), reverse=True)
 
 
 class Net:
@@ -350,12 +358,6 @@
         n = 6 if a else 7
         there = p1.at[pl.ds(0, n), pl.ds(1 - a, 1), :, pl.ds(4 * zslot(k), 4)]
         send(c1_copies, p1.at[pl.ds(0, n), pl.ds(1, 1), :, pl.ds(0, 4)], there, (k, a, 0))
-    pl.semaphore_wait(go_c, 2)
-    for k, a in [(0, 0)] + ZX:
-        for t in (1, -1):
-            there = s1l if t == 1 else s1h
-            send(c1_copies, s1.at[:, pl.ds(0, 4)], there.at[1 - a, :, pl.ds(4 * zslot(k), 4)], (k, a, t))
-
     level2 = [right(left(rows12(PICKS[q][0], PICKS[q][1]), level1[q]), lanes12(PICKS[q][2])) for q in range(7)]
     level3 = [right(left(rows23(PICKS[q][0], PICKS[q][1]), level2[q]), lanes23(PICKS[q][2])) for q in range(7)]
     inside2 = (ly >= 32) & (ly < 64) & (sx < 4)
@@ -447,11 +449,16 @@
         b1c[1, 1, x, 0:4, :] = rhs1[4 * x : 4 * x + 4]
 
     r2 = net.group()
-    for t in (0, 1, -1):
-        for k, a in [(0, 0)] + ZX:
-            if (k, a, t) != (0, 0, 0):
-                there = b1c.at[1 - t, 1 - a, :, pl.ds(4 * zslot(k), 4)]
-                send(r2, b1c.at[1, 1, :, pl.ds(0, 4)], there, (k, a, t))
+    for k, a, t in NEAR_27:
+        if (k, a, t) != (0, 0, 0):
+            there = b1c.at[1 - t, 1 - a, :, pl.ds(4 * zslot(k), 4)]
+            send(r2, b1c.at[1, 1, :, pl.ds(0, 4)], there, (k, a, t))
+
+    pl.semaphore_wait(go_c, 2)
+    for k, a in [(0, 0)] + ZX:
+        for t in (1, -1):
+            there = s1l if t == 1 else s1h
+            send(c1_copies, s1.at[:, pl.ds(0, 4)], there.at[1 - a, :, pl.ds(4 * zslot(k), 4)], (k, a, t))
 
     pack = jnp.zeros((8, 128), F32)
     for z in range(8):
@@ -521,12 +528,12 @@
         b2r[x] = roll(rhs2, 32, 1) + roll(rhs2, -32, 1)
 
     r3 = net.group()
-    for a in (0, 1, -1, 2, -2, 3, -3):
+    for a in (3, -3, 2, -2, 1, -1, 0):
         there = pl.ds(xplace(6, 2, a), 2)
-        if a:
-            send(r3, b2c.at[pl.ds(6, 2)], b2c.at[there], (0, a, 0))
         send(r3, b2r, b2l.at[there], (0, a, 1))
         send(r3, b2r, b2h.at[there], (0, a, -1))
+    for a in (3, -3, 2, -2, 1, -1):
+        send(r3, b2c.at[pl.ds(6, 2)], b2c.at[pl.ds(xplace(6, 2, a), 2)], (0, a, 0))
     pl.semaphore_wait(go_b, 2)
     c3_copies = net.group()
     for a in range(1, 16):
@@ -550,7 +557,7 @@
     b3[0] = rhs3
 
     r4 = net.group()
-    for a in range(1, 16):
+    for a in ALONG_X:
         send(r4, b3.at[pl.ds(0, 1)], b3.at[pl.ds(16 - a, 1)], (0, a, 0))
     wait(c3_copies)
     terms3 = []

time: 44.2 us -> 43.1 us (0.975)
  Pallas kernels: 42.6 us -> 41.5 us
    pallas_call x1, Pallas kernels: 42.6 us -> 41.5 us  [on_device(): pl.pallas_call(kernel, out_shape=jax.ShapeDtypeStruct((8, 8, 128), F32),...]
where the time goes in v5:
time: 43.1 us; the launch traced here: 42.9 us
  Pallas kernels  41.5 us (96%)
  local copies, waits for them, and re-layouts  1.38 us (3%)
    pallas_call x1, Pallas kernels, on_device(): pl.pallas_call(kernel, out_shape=jax.ShapeDtypeStruct((8, 8, 128), F32),...  41.5 us
    unnamed x1, local copies, waits for them, and re-layouts  1.38 us

profile of v5, /device:TPU:1, one launch (start us, length us, event | category | flops | bytes accessed | tf_op | source)
XLA Modules:
  0.0 42.9 jit_solution(4339862463991419671)
XLA Ops:
  0.0 41.5 %shard_map.55 = f32[8,8,128]{2,1,0:T(8,128)} custom-call(f32[8,8,128]{2,1,0:T(8,128)} %src_hbm.1, f32[8,8,128]{2,1,0:T(8,128)} %r_hbm.1, f32[3,8,8,128]{3,2,1,0:T(8,128)} %k_hbm.1, f32[3,8,8,128]{3,2,1,0:T(8,128)} %v_hbm.1, s32[3,8,8,128]{3,2,1,0:T(8,128)} %f_hbm.1), custom_call_target="tpu_custom_call" | custom-call | tf_op jit(solution)/shard_map/pallas_call | solution.py:657
  41.6 1.4 %copy.7 = f32[8,8,128]{2,1,0:T(8,128)} copy(f32[8,8,128]{2,1,0:T(8,128)} %shard_map.55) | data formatting | bytes 65536

commit v6 on v5

--- a/solution.py
+++ b/solution.py
@@ -80,7 +80,7 @@
 
 
 def mat(rows, cols, where):
-    return jnp.where(where(iota((rows, cols), 0), iota((rows, cols), 1)), 1.0, 0.0).astype(F32)
+    return jnp.where(where(iota((rows, cols), 0), iota((rows, cols), 1)), 1.0, 0.0).astype(jnp.bfloat16)
 
 
 def split(x):
@@ -382,6 +382,7 @@
                 send(z_copies, a2.at[pl.ds(1, 1), :, pl.ds(0, 2)], there, (k, 0, t))
                 send(z_copies, a3.at[pl.ds(1, 1), pl.ds(0, 1)], a3.at[pl.ds(1 - t, 1), pl.ds(zslot(k), 1)], (k, 0, t))
 
+    rows_r1, lanes_r1 = rows01(None), lanes01(None)
     wait(r1)
     pl.semaphore_wait(go_a, 2)
     for a in (4, -4):
@@ -443,7 +444,7 @@
     for z in range(4):
         two = [(sweep_a(va, vx, vy, 2 + p, 2) - va[2 + p]) * d0[p] for p in (2 * z, 2 * z + 1)]
         planes.append(two[0] + two[1])
-    rhs1 = right(left(rows01(None), jnp.concatenate(planes, axis=0)), lanes01(None))
+    rhs1 = right(left(rows_r1, jnp.concatenate(planes, axis=0)), lanes_r1)
     rhs1 = halves(jnp.where(own1, rhs1 / jnp.where(own1, d1_own, 1.0), 0.0))
     for x in range(2):
         b1c[1, 1, x, 0:4, :] = rhs1[4 * x : 4 * x + 4]
@@ -506,6 +507,7 @@
         block = p1[6, 1, x]
         c1[6, 4 + x] = block
         c1[6, 6 + x] = roll(block, 64, 1)
+    halve, lanes_r2 = mat(8, 16, lambda i, j: (j >> 1) == i), lanes12(None)
     wait(r2)
     for i in range(3):
         for x in range(2):
@@ -518,8 +520,7 @@
     for x in range(2):
         two = [(sweep_l(v1p, b1, c1, p) - v1p[p]) * c1[6, p] for p in (4 + 2 * x, 5 + 2 * x)]
         rows.append(two[0] + two[1])
-    rows = right(jnp.concatenate(rows, axis=0), lanes12(None))
-    halve = mat(8, 16, lambda i, j: (j >> 1) == i)
+    rows = right(jnp.concatenate(rows, axis=0), lanes_r2)
     for x in range(2):
         inside = (ly >= 32) & (ly < 64)
         rhs2 = left(halve, rows[16 * x : 16 * x + 16])
@@ -540,14 +541,16 @@
         send(c3_copies, c3.at[:, pl.ds(0, 1), pl.ds(0, 4)], c3.at[:, pl.ds(16 - a, 1), pl.ds(0, 4)], (0, a, 0))
 
     wait(c2_copies)
+    lanes_r3 = mat(128, 128, lambda i, j: (j == (i >> 1)) & (i < 96))
+    rows_r3 = mat(8, 8, lambda i, j: (j >> 1) == (i & 3))
     wait(r3)
     for x in range(14):
         b2[x] = jnp.where(ly < 32, b2l[x], jnp.where(ly >= 64, b2h[x], b2c[x]))
     for x in range(2, 12):
         v2p[x] = sweep_l(b2, b2, c2, x)
     two = [(sweep_l(v2p, b2, c2, p) - v2p[p]) * c2[6, p] for p in (6, 7)]
-    rows = right(two[0] + two[1], mat(128, 128, lambda i, j: (j == (i >> 1)) & (i < 96)))
-    rhs3 = left(mat(8, 8, lambda i, j: (j >> 1) == (i & 3)), rows)
+    rows = right(two[0] + two[1], lanes_r3)
+    rhs3 = left(rows_r3, rows)
 
     def twice(block):
         return jnp.where(sx < 4, block, roll(block, 4, 0))
@@ -564,6 +567,22 @@
     for q in range(3):
         terms3.append([twice(c3[q, x]) for x in range(16)])
         terms3.append([roll(block, 64, 1) for block in terms3[-1]])
+    def lanes10(i, j):
+        main = (j < 128) & (i == 32 + (j >> 1))
+        return main | ((j >= 254) & (i == 31)) | ((j >= 128) & (j < 130) & (i == 96))
+
+    def rows10(i, j):
+        xi, zr = j >> 4, j & 15
+        main = (i < 96) & (zr == (((i >> 4) + 15) & 15)) & (xi == 1 + ((i & 7) >> 1))
+        n = i - 96
+        beside = (i >= 96) & (zr == ((((n >> 3) + 31) >> 1) & 15)) & (
+            (((n & 7) >= 6) & (xi == 0)) | (((n & 7) < 2) & (xi == 5))
+        )
+        return main | beside
+
+    rows_32, lanes_32 = mat(8, 8, lambda i, j: j == (i >> 1)), mat(128, 128, lambda i, j: (i == (j >> 1)) & (j < 96))
+    rows_21, lanes_21 = mat(16, 8, lambda i, j: j == (i >> 1)), mat(128, 128, lambda i, j: i == 16 + (j >> 1))
+    rows_10, lanes_10 = mat(176, 96, rows10), mat(128, 256, lanes10)
     wait(r4)
     rhs3 = [b3[x] for x in range(16)]
     here = rhs3
@@ -576,9 +595,9 @@
             for x in range(16)
         ]
 
-    wide = left(mat(8, 8, lambda i, j: j == (i >> 1)), jnp.concatenate([here[(X + 16) % 16] for X in range(-2, 3)], axis=1))
+    wide = left(rows_32, jnp.concatenate([here[(X + 16) % 16] for X in range(-2, 3)], axis=1))
     wide = jnp.concatenate([wide[:, 128 * i : 128 * i + 128] for i in range(5)], axis=0)
-    wide = right(wide, mat(128, 128, lambda i, j: (i == (j >> 1)) & (j < 96)))
+    wide = right(wide, lanes_32)
     for x in range(2, 12):
         i = (x >> 1) - 1
         v2p[x] = v2p[x] + wide[8 * i : 8 * i + 8]
@@ -586,8 +605,8 @@
         v2q[x] = sweep_l(v2p, b2, c2, x)
     ups = [sweep_l(v2q, b2, c2, x) for x in range(4, 10)]
 
-    wide = right(jnp.concatenate(ups, axis=0), mat(128, 128, lambda i, j: i == 16 + (j >> 1)))
-    wide = left(mat(16, 8, lambda i, j: j == (i >> 1)), jnp.concatenate([wide[8 * i : 8 * i + 8] for i in range(6)], axis=1))
+    wide = right(jnp.concatenate(ups, axis=0), lanes_21)
+    wide = left(rows_21, jnp.concatenate([wide[8 * i : 8 * i + 8] for i in range(6)], axis=1))
     for x in range(1, 11):
         i = x >> 1
         v1p[x] = v1p[x] + wide[:, 128 * i : 128 * i + 128]
@@ -595,21 +614,8 @@
         v1q[x] = sweep_l(v1p, b1, c1, x)
     ups = [sweep_l(v1q, b1, c1, x) for x in range(3, 9)]
 
-    def lanes10(i, j):
-        main = (j < 128) & (i == 32 + (j >> 1))
-        return main | ((j >= 254) & (i == 31)) | ((j >= 128) & (j < 130) & (i == 96))
-
-    def rows10(i, j):
-        xi, zr = j >> 4, j & 15
-        main = (i < 96) & (zr == (((i >> 4) + 15) & 15)) & (xi == 1 + ((i & 7) >> 1))
-        n = i - 96
-        beside = (i >= 96) & (zr == ((((n >> 3) + 31) >> 1) & 15)) & (
-            (((n & 7) >= 6) & (xi == 0)) | (((n & 7) < 2) & (xi == 5))
-        )
-        return main | beside
-
-    wide = right(jnp.concatenate(ups, axis=0), mat(128, 256, lanes10))
-    wide = left(mat(176, 96, rows10), wide)
+    wide = right(jnp.concatenate(ups, axis=0), lanes_10)
+    wide = left(rows_10, wide)
     wait(up0)
     low = (ly & 2) == 0
     beside = jnp.where(low, wpkr[0], wpkr[1])

time: 43.1 us -> 43.1 us (level)
  no operation moved by 1% of the time
where the time goes in v6:
time: 43.1 us; the launch traced here: 42.9 us
  Pallas kernels  41.5 us (96%)
  local copies, waits for them, and re-layouts  1.38 us (3%)
    pallas_call x1, Pallas kernels, on_device(): pl.pallas_call(kernel, out_shape=jax.ShapeDtypeStruct((8, 8, 128), F32),...  41.5 us
    unnamed x1, local copies, waits for them, and re-layouts  1.38 us

profile of v6, /device:TPU:1, one launch (start us, length us, event | category | flops | bytes accessed | tf_op | source)
XLA Modules:
  0.0 42.9 jit_solution(5827517875828719291)
XLA Ops:
  0.0 41.5 %shard_map.55 = f32[8,8,128]{2,1,0:T(8,128)} custom-call(f32[8,8,128]{2,1,0:T(8,128)} %src_hbm.1, f32[8,8,128]{2,1,0:T(8,128)} %r_hbm.1, f32[3,8,8,128]{3,2,1,0:T(8,128)} %k_hbm.1, f32[3,8,8,128]{3,2,1,0:T(8,128)} %v_hbm.1, s32[3,8,8,128]{3,2,1,0:T(8,128)} %f_hbm.1), custom_call_target="tpu_custom_call" | custom-call | tf_op jit(solution)/shard_map/pallas_call | solution.py:663
  41.5 1.4 %copy.7 = f32[8,8,128]{2,1,0:T(8,128)} copy(f32[8,8,128]{2,1,0:T(8,128)} %shard_map.55) | data formatting | bytes 65536
